TPU v7x, 32 devices: a whole 2x2x4 slice. The times are simulated.
32 devices in a mesh: dp: 8 (over z, y), section: 2 (over x), mp: 2 (over core).
Axes of the slice: x: 2, y: 2, z: 4, core: 2. Of those that a mesh axis runs over, the one named last changes fastest.
Arguments:
- enc_input: bfloat16 [8, 2, 64, 4096], P('dp', None, 'mp'), may hold values from -6 to 6
- dec_input: bfloat16 [8, 2, 64, 4096], P('dp', None, 'mp'), may hold values from -6 to 6
- enc_lengths: int32 [8, 2, 3], P('dp'), may hold values from 1 to 32, 64 in all within a row
- dec_lengths: int32 [8, 2, 3], P('dp'), may hold values from 1 to 32, 64 in all within a row
- w_query: bfloat16 [2, 4096, 2048], P('section', 'dp', 'mp'), may hold values from -0.09375 to 0.09375
- w_key: bfloat16 [2, 4096, 2048], P('section', 'dp', 'mp'), may hold values from -0.09375 to 0.09375
- w_value: bfloat16 [2, 4096, 2048], P('section', 'dp', 'mp'), may hold values from -0.09375 to 0.09375
- w_output: bfloat16 [2, 2048, 4096], P('section', 'mp', 'dp'), may hold values from -0.125 to 0.125
- layer_gains: float32 [2, 4096], P('section'), may hold values from 0.1 to 1.9
- final_gain: float32 [4096], replicated, may hold values from 0.1 to 1.9
- cotangent: bfloat16 [8, 2, 64, 4096], P('dp', None, 'mp'), may hold values from -6 to 6
Outputs:
- layer_outputs: bfloat16 [2, 8, 2, 64, 4096], P('section', 'dp', None, 'mp')
- input_grads: bfloat16 [2, 8, 2, 64, 4096], P('section', 'dp', None, 'mp')
- gain_grads: float32 [2, 4096], P('section')
- final_grad: float32 [4096], replicated
Inputs may be any that keep to these rules, and one draw needn't show every extreme that they name: `enc_lengths`: each row of lengths sums to 64; every row's largest length is exactly 32. `dec_lengths`: each row of lengths sums to 64; every row's largest length is exactly 32.
All inputs are finite; a program needn't handle non-finite values.
Results may differ from a plain program's by a relative error of at most 0.019.
Values may be sent and summed in bfloat16 or wider, within the bound.
A program may use at most 128 MiB of HBM per device.

v0:
```python
import jax
import jax.numpy as jnp
from jax import lax
from jax.sharding import PartitionSpec as P

HD = 256


epsilon = 1e-06


def broadcast(block, axis, source):
    block = jnp.where(lax.axis_index(axis) == source, block, jnp.zeros_like(block))
    return lax.psum(block, axis)


def rounded(array):
    return lax.optimization_barrier(array.astype(jnp.bfloat16)).astype(jnp.float32)


def segment_ids(lengths, count):
    ends = jnp.cumsum(lengths, axis=-1)
    position = jnp.arange(count, dtype=jnp.int32)
    above = (position[None, :, None] >= ends[:, None, :-1]).astype(jnp.int32)
    return jnp.sum(above, axis=-1)


def rms_norm(inputs, norm_gain):
    floats = inputs.astype(jnp.float32)
    spread = jnp.sqrt(jnp.mean(floats * floats, axis=-1, keepdims=True) + epsilon)
    normal = floats / spread
    return (normal * norm_gain, normal, spread)


def norm_back(grad_out, normal, spread, norm_gain):
    scaled = grad_out * norm_gain
    return (scaled - normal * jnp.mean(scaled * normal, axis=-1, keepdims=True)) / spread


def attend(hidden, source, w_query, w_key, w_value, w_output, seg_query, seg_key, head_size):
    row_count = hidden.shape[0]
    query = rounded(jnp.dot(hidden, w_query, preferred_element_type=jnp.float32))
    key_rows = rounded(jnp.dot(source, w_key, preferred_element_type=jnp.float32))
    value_rows = rounded(jnp.dot(source, w_value, preferred_element_type=jnp.float32))
    query_heads = query.reshape(row_count, -1, head_size)
    key_heads = key_rows.reshape(row_count, -1, head_size)
    value_heads = value_rows.reshape(row_count, -1, head_size)
    scores = jnp.einsum("qhd,khd->hqk", query_heads, key_heads) * head_size ** (-0.5)
    same_doc = seg_query[:, None] == seg_key[None, :]
    scores = jnp.where(same_doc[None], scores, -1e30)
    row_max = jnp.max(scores, axis=-1, keepdims=True)
    exponent = jnp.exp(scores - row_max)
    attention = exponent / jnp.sum(exponent, axis=-1, keepdims=True)
    mixed = jnp.einsum("hqk,khd->qhd", rounded(attention), value_heads).reshape(row_count, -1)
    partial_value = jnp.dot(
        mixed.astype(jnp.bfloat16), w_output, preferred_element_type=jnp.float32
    )
    return (partial_value, (query, key_rows, value_rows, attention))


def attend_back(grad_in, stored, w_query, w_key, w_value, w_output, head_size):
    query, key_rows, value_rows, attention = stored
    row_count = grad_in.shape[0]
    scale = head_size ** (-0.5)
    grad_mixed = rounded(jnp.dot(grad_in, w_output.T, preferred_element_type=jnp.float32))
    grad_heads = grad_mixed.reshape(row_count, -1, head_size)
    query_heads = query.reshape(row_count, -1, head_size)
    key_heads = key_rows.reshape(row_count, -1, head_size)
    value_heads = value_rows.reshape(row_count, -1, head_size)
    grad_value = rounded(jnp.einsum("hqk,qhd->khd", rounded(attention), grad_heads)).reshape(
        row_count, -1
    )
    grad_att = jnp.einsum("qhd,khd->hqk", grad_heads, value_heads)
    grad_scores = (
        attention * (grad_att - jnp.sum(attention * grad_att, axis=-1, keepdims=True)) * scale
    )
    grad_query = rounded(jnp.einsum("hqk,khd->qhd", grad_scores, key_heads)).reshape(row_count, -1)
    grad_key = rounded(jnp.einsum("hqk,qhd->khd", grad_scores, query_heads)).reshape(row_count, -1)
    grad_hidden = jnp.dot(
        grad_query.astype(jnp.bfloat16), w_query.T, preferred_element_type=jnp.float32
    )
    grad_source = jnp.dot(
        grad_key.astype(jnp.bfloat16), w_key.T, preferred_element_type=jnp.float32
    )
    grad_source = grad_source + jnp.dot(
        grad_value.astype(jnp.bfloat16), w_value.T, preferred_element_type=jnp.float32
    )
    return (grad_hidden, grad_source)


def shards(
    enc_input,
    dec_input,
    enc_lengths,
    dec_lengths,
    w_query,
    w_key,
    w_value,
    w_output,
    layer_gains,
    final_gain,
    cotangent,
):
    section_count = lax.axis_size("section")
    first_dec = max(1, section_count * 3 // 8)
    section_index = lax.axis_index("section")
    is_encoder = section_index < first_dec
    micro_count = enc_input.shape[1]
    piece_rows = enc_input.shape[2]
    row_count = piece_rows * lax.axis_size("mp")
    model_width = enc_input.shape[3]
    enc_seg = segment_ids(enc_lengths[0], row_count)
    dec_seg = segment_ids(dec_lengths[0], row_count)
    entry_rows = jnp.where(is_encoder, enc_input[0], dec_input[0])
    norm_gain = layer_gains[0]
    gathered = (
        lax.all_gather(w_query, "dp", axis=1, tiled=True),
        lax.all_gather(w_key, "dp", axis=1, tiled=True),
        lax.all_gather(w_value, "dp", axis=1, tiled=True),
        lax.all_gather(w_output, "dp", axis=2, tiled=True),
    )
    layer_params = (norm_gain, gathered[0][0], gathered[1][0], gathered[2][0], gathered[3][0])
    local_width = layer_params[1].shape[1]
    heads_local = local_width // HD

    def layer_forward(inputs_piece, source_rows, seg_query, seg_key, is_valid, params):
        inputs = lax.all_gather(inputs_piece, "mp", axis=0, tiled=True)

        def layer_compute(operands):
            layer_in, source_in, query_seg, key_seg = operands
            hidden = rms_norm(layer_in, params[0])[0].astype(jnp.bfloat16)
            source = jnp.where(is_encoder, hidden, source_in)
            return attend(
                hidden, source, params[1], params[2], params[3], params[4], query_seg, key_seg, HD
            )

        def layer_skip(operands):
            zero_rows = jnp.zeros((row_count, local_width), jnp.float32)
            zero_att = jnp.zeros((heads_local, row_count, row_count), jnp.float32)
            return (
                jnp.zeros((row_count, model_width), jnp.float32),
                (zero_rows, zero_rows, zero_rows, zero_att),
            )

        partial_value, stored = lax.cond(
            is_valid, layer_compute, layer_skip, (inputs, source_rows, seg_query, seg_key)
        )
        summed = lax.psum_scatter(
            partial_value.astype(jnp.bfloat16), "mp", scatter_dimension=0, tiled=True
        ).astype(jnp.float32)
        result = (inputs_piece.astype(jnp.float32) + summed).astype(jnp.bfloat16)
        return (result, inputs, stored)

    def forward_step(step, carry, position, active, encoded_rows, params):
        layer_out, saved_inputs, saved_query, saved_key, saved_value, saved_att = carry
        raw = step - position
        is_valid = active & (raw >= 0) & (raw < micro_count)
        slot = jnp.clip(raw, 0, micro_count - 1)
        inputs_piece = entry_rows[slot]
        seg_query = jnp.where(is_encoder, enc_seg[slot], dec_seg[slot])
        result, inputs, stored = layer_forward(
            inputs_piece, encoded_rows[slot], seg_query, enc_seg[slot], is_valid, params
        )

        def keep(table, value):
            return table.at[slot].set(jnp.where(is_valid, value, table[slot]))

        layer_out = keep(layer_out, result)
        saved_inputs = keep(saved_inputs, inputs)
        saved_query = keep(saved_query, stored[0])
        saved_key = keep(saved_key, stored[1])
        saved_value = keep(saved_value, stored[2])
        saved_att = keep(saved_att, stored[3])
        return ((layer_out, saved_inputs, saved_query, saved_key, saved_value, saved_att), result)

    rows_zero = jnp.zeros((micro_count, row_count, model_width), jnp.bfloat16)
    pieces_zero = jnp.zeros((micro_count, piece_rows, model_width), jnp.bfloat16)
    heads_zero = jnp.zeros((micro_count, row_count, local_width), jnp.float32)
    start = (
        pieces_zero,
        rows_zero,
        heads_zero,
        heads_zero,
        heads_zero,
        jnp.zeros((micro_count, heads_local, row_count, row_count), jnp.float32),
    )
    carry = lax.fori_loop(
        0,
        first_dec + micro_count - 1,
        lambda step, state: forward_step(
            step, state, section_index, is_encoder, rows_zero, layer_params
        )[0],
        start,
    )
    encoded = broadcast(carry[0], "section", first_dec - 1)
    normed = rms_norm(encoded, final_gain)[0].astype(jnp.bfloat16)
    encoded_rows = lax.all_gather(normed, "mp", axis=1, tiled=True)
    carry = lax.fori_loop(
        0,
        section_count - first_dec + micro_count - 1,
        lambda step, state: forward_step(
            step,
            state,
            section_index - first_dec,
            jnp.logical_not(is_encoder),
            encoded_rows,
            layer_params,
        )[0],
        carry,
    )
    layer_out = carry[0]
    saved_inputs, saved_query, saved_key, saved_value, saved_att = (
        carry[1],
        carry[2],
        carry[3],
        carry[4],
        carry[5],
    )
    enc_normal, enc_spread = rms_norm(encoded, final_gain)[1:]

    def backward_step(step, carry, position, active, entry_grads, params):
        grads, cross, gain_sum = carry
        raw = step - position
        is_valid = active & (raw >= 0) & (raw < micro_count)
        slot = jnp.clip(raw, 0, micro_count - 1)
        grad_piece = entry_grads[slot]
        grad_in = lax.all_gather(grad_piece, "mp", axis=0, tiled=True)

        def backward_compute(operands):
            grad_rows, layer_in, stored = operands
            normal, spread = rms_norm(layer_in, params[0])[1:]
            grad_hidden, grad_source = attend_back(
                grad_rows, stored, params[1], params[2], params[3], params[4], HD
            )
            grad_hidden = grad_hidden + jnp.where(is_encoder, grad_source, 0.0)
            grad_inputs = rounded(norm_back(grad_hidden, normal, spread, params[0]))
            return (
                grad_inputs,
                jnp.where(is_encoder, 0.0, grad_source),
                jnp.sum(grad_hidden * normal, axis=0),
            )

        def backward_skip(operands):
            zero_rows = jnp.zeros((row_count, model_width), jnp.float32)
            return (zero_rows, zero_rows, jnp.zeros((model_width,), jnp.float32))

        stored = (saved_query[slot], saved_key[slot], saved_value[slot], saved_att[slot])
        grad_part, grad_source, gain_part = lax.cond(
            is_valid, backward_compute, backward_skip, (grad_in, saved_inputs[slot], stored)
        )
        summed = lax.psum_scatter(
            grad_part.astype(jnp.bfloat16), "mp", scatter_dimension=0, tiled=True
        ).astype(jnp.float32)
        result = (grad_piece.astype(jnp.float32) + summed).astype(jnp.bfloat16)
        grads = grads.at[slot].set(jnp.where(is_valid, result, grads[slot]))
        cross = cross.at[slot].add(grad_source)
        gain_sum = gain_sum + gain_part
        return (grads, cross, gain_sum)

    back_start = (
        pieces_zero,
        jnp.zeros((micro_count, row_count, model_width), jnp.float32),
        jnp.zeros((model_width,), jnp.float32),
    )
    carry = lax.fori_loop(
        0,
        section_count - first_dec + micro_count - 1,
        lambda step, state: backward_step(
            step,
            state,
            section_count - 1 - section_index,
            jnp.logical_not(is_encoder),
            cotangent[0],
            layer_params,
        ),
        back_start,
    )
    cross_total = lax.psum(carry[1].astype(jnp.bfloat16), ("section", "mp")).astype(jnp.float32)
    row_start = lax.axis_index("mp") * piece_rows
    cross_piece = lax.dynamic_slice_in_dim(cross_total, row_start, piece_rows, 1)
    enc_grads = norm_back(cross_piece, enc_normal, enc_spread, final_gain).astype(jnp.bfloat16)
    final_part = jnp.sum(cross_piece * enc_normal, axis=(0, 1))
    carry = lax.fori_loop(
        0,
        first_dec + micro_count - 1,
        lambda step, state: backward_step(
            step, state, first_dec - 1 - section_index, is_encoder, enc_grads, layer_params
        ),
        carry,
    )
    gain_total = lax.psum(carry[2], ("dp", "mp"))
    final_total = lax.psum(final_part, ("dp", "mp"))
    return (layer_out[None, None], carry[0][None, None], gain_total[None], final_total)


def solution(mesh):
    return jax.shard_map(
        shards,
        mesh=mesh,
        in_specs=(
            P("dp", None, "mp", None),
            P("dp", None, "mp", None),
            P("dp", None, None),
            P("dp", None, None),
            P("section", "dp", "mp"),
            P("section", "dp", "mp"),
            P("section", "dp", "mp"),
            P("section", "mp", "dp"),
            P("section", None),
            P(),
            P("dp", None, "mp", None),
        ),
        out_specs=(
            P("section", "dp", None, "mp", None),
            P("section", "dp", None, "mp", None),
            P("section", None),
            P(),
        ),
        check_vma=False,
    )
```

profile of v0, /device:TPU:0, one launch (start us, length us, event | category | flops | bytes accessed | tf_op | source)
XLA Modules:
  0.0 1002.8 jit_solution(11415209342300622380)
XLA Ops:
  13.5 124.3 %all-gather.19.cloned.1.call-done = bf16[1,4096,1024]{2,1,0:T(8,128)(2,1)} async-done(((bf16[1,512,1024]{2,1,0:T(8,128)(2,1)}), bf16[1,4096,1024]{2,1,0:T(8,128)(2,1)}) %all-gather.19.cloned.1.call-update) | async-done | bytes 8388624 | tf_op jit(solution)/shard_map/all_gather | solution.py:119
  137.8 125.3 %all-gather.21.cloned.1.call-done = bf16[1,4096,1024]{2,1,0:T(8,128)(2,1)} async-done(((bf16[1,512,1024]{2,1,0:T(8,128)(2,1)}), bf16[1,4096,1024]{2,1,0:T(8,128)(2,1)}) %all-gather.21.cloned.1.call-update) | async-done | bytes 8388624 | tf_op jit(solution)/shard_map/all_gather | solution.py:117
  263.1 125.3 %all-gather.23.cloned.1.call-done = bf16[1,4096,1024]{2,1,0:T(8,128)(2,1)} async-done(((bf16[1,512,1024]{2,1,0:T(8,128)(2,1)}), bf16[1,4096,1024]{2,1,0:T(8,128)(2,1)}) %all-gather.23.cloned.1.call-update) | async-done | bytes 8388624 | tf_op jit(solution)/shard_map/all_gather | solution.py:118
  388.4 125.5 %all-gather.25.cloned.1.call-done = bf16[1,1024,4096]{2,1,0:T(8,128)(2,1)} async-done(((bf16[1,1024,512]{2,1,0:T(8,128)(2,1)}), bf16[1,1024,4096]{2,1,0:T(8,128)(2,1)}) %all-gather.25.cloned.1.call-update) | async-done | bytes 8388624 | tf_op jit(solution)/shard_map/all_gather | solution.py:120
  517.0 76.5 %while.100 = (s32[]{:T(128)}, bf16[2,32,4096]{2,1,0:T(8,128)(2,1)}, bf16[2,64,4096]{2,1,0:T(8,128)(2,1)S(1)}, bf16[2,64,1024]{2,1,0:T(8,128)(2,1)}, bf16[2,64,10...) while((s32[]{:T(128)}, bf16[2,32,4096]{2,1,0:T(8,128)(2,1)}, ...), condition=%wide.region_13.14_spmd, body=%wide.region_4.13_spmd.sunk | while | flops 2170818560 | bytes 77202120 | solution.py:187
  519.3 20.5 %conditional.9 = (bf16[64,4096]{1,0:T(8,128)(2,1)S(1)}, bf16[64,1024]{1,0:T(8,128)(2,1)S(1)}, bf16[64,1024]{1,0:T(8,128)(2,1)}, bf16[64,1024]{1,0:T(8,128)(2,1)}, f32[4,64,64]{1,2,0:T(8,128)S(1)}) conditional(s32[]{:T(128)} %convert_element_type.700, () %tuple.329, (pred[]{:T(512)}, bf16[64,4096]{1,0:T(8,128)(2,1)S(1)}, f32[1,4096]{1,0:T(1,128)S(1)}, ...), branch_computations={%region_6.6_spmd, %region_7.10_spmd} | conditional | flops 2169081856 | bytes 64550064 | solution.py:145
  557.5 20.5 %conditional.9 = (bf16[64,4096]{1,0:T(8,128)(2,1)S(1)}, bf16[64,1024]{1,0:T(8,128)(2,1)S(1)}, bf16[64,1024]{1,0:T(8,128)(2,1)}, bf16[64,1024]{1,0:T(8,128)(2,1)}, f32[4,64,64]{1,2,0:T(8,128)S(1)}) conditional(s32[]{:T(128)} %convert_element_type.700, () %tuple.329, (pred[]{:T(512)}, bf16[64,4096]{1,0:T(8,128)(2,1)S(1)}, f32[1,4096]{1,0:T(1,128)S(1)}, ...), branch_computations={%region_6.6_spmd, %region_7.10_spmd} | conditional | flops 2169081856 | bytes 64550064 | solution.py:145
  595.7 27.5 %all-reduce.4.cloned.1.call-done = bf16[2,32,4096]{2,1,0:T(8,128)(2,1)} async-done(((bf16[2,32,4096]{2,1,0:T(8,128)(2,1)}), bf16[2,32,4096]{2,1,0:T(8,128)(2,1)}) %all-reduce.4.cloned.1.call-update) | async-done | bytes 524304 | tf_op jit(solution)/shard_map/psum | solution.py:14
  626.5 9.2 all-gather.27.cloned.1.call-done
  635.7 74.1 %while.101 = (s32[]{:T(128)}, bf16[2,32,4096]{2,1,0:T(8,128)(2,1)}, bf16[2,64,4096]{2,1,0:T(8,128)(2,1)S(1)}, bf16[2,64,1024]{2,1,0:T(8,128)(2,1)}, bf16[2,64,10...) while((s32[]{:T(128)}, bf16[2,32,4096]{2,1,0:T(8,128)(2,1)}, ...), condition=%wide.region_25.26_spmd, body=%wide.region_16.25_spmd.sunk | while | flops 2170818560 | bytes 78252760 | solution.py:198
  650.7 18.2 %reduce-scatter.7.cloned.1.call-done = bf16[32,4096]{1,0:T(8,128)(2,1)} async-done(((bf16[64,4096]{1,0:T(8,128)(2,1)}), bf16[32,4096]{1,0:T(8,128)(2,1)}) %reduce-scatter.7.cloned.1.call-update) | async-done | bytes 262160 | tf_op jit(solution)/shard_map/while/body/eval_jaxpr/reduce_scatter | solution.py:148
  686.1 21.4 %reduce-scatter.7.cloned.1.call-done = bf16[32,4096]{1,0:T(8,128)(2,1)} async-done(((bf16[64,4096]{1,0:T(8,128)(2,1)}), bf16[32,4096]{1,0:T(8,128)(2,1)}) %reduce-scatter.7.cloned.1.call-update) | async-done | bytes 262160 | tf_op jit(solution)/shard_map/while/body/eval_jaxpr/reduce_scatter | solution.py:148
  712.2 91.7 %while.103 = (s32[]{:T(128)}, bf16[2,32,4096]{2,1,0:T(8,128)(2,1)}, f32[2,64,4096]{2,1,0:T(8,128)}, f32[4096]{0:T(1024)}, s32[]{:T(128)}, /*index=5*/pred[]{:T(5...) while((s32[]{:T(128)}, bf16[2,32,4096]{2,1,0:T(8,128)(2,1)}, ...), condition=%wide.region_35.36_spmd.clone, body=%wide.region_26.35_spmd.clone.sunk | while | flops 2188119808 | bytes 58795800 | solution.py:265
  723.5 33.6 %reduce-scatter.11.cloned.1.call-done = bf16[32,4096]{1,0:T(8,128)(2,1)} async-done(((bf16[64,4096]{1,0:T(8,128)(2,1)}), bf16[32,4096]{1,0:T(8,128)(2,1)}) %reduce-scatter.11.cloned.1.call-update) | async-done | bytes 262160 | tf_op jit(solution)/shard_map/while/body/eval_jaxpr/reduce_scatter | solution.py:251
  771.0 30.4 %reduce-scatter.11.cloned.1.call-done = bf16[32,4096]{1,0:T(8,128)(2,1)} async-done(((bf16[64,4096]{1,0:T(8,128)(2,1)}), bf16[32,4096]{1,0:T(8,128)(2,1)}) %reduce-scatter.11.cloned.1.call-update) | async-done | bytes 262160 | tf_op jit(solution)/shard_map/while/body/eval_jaxpr/reduce_scatter | solution.py:251
  806.6 37.9 %all-reduce.6.cloned.1.call-done = bf16[2,64,4096]{2,1,0:T(8,128)(2,1)} async-done(((bf16[2,64,4096]{2,1,0:T(8,128)(2,1)}), bf16[2,64,4096]{2,1,0:T(8,128)(2,1)}) %all-reduce.6.cloned.1.call-update) | async-done | bytes 1048592 | tf_op jit(solution)/shard_map/psum | solution.py:278
  848.5 85.3 %while.102 = (s32[]{:T(128)}, bf16[2,32,4096]{2,1,0:T(8,128)(2,1)}, f32[4096]{0:T(1024)}, s32[]{:T(128)}, pred[]{:T(512)}, /*index=5*/bf16[2,32,4096]{2,1,0:T(8,...) while((s32[]{:T(128)}, bf16[2,32,4096]{2,1,0:T(8,128)(2,1)}, ...), condition=%wide.region_47.48_spmd, body=%wide.region_38.0_spmd.sunk | while | flops 2187329280 | bytes 55780248 | solution.py:283
  851.6 27.9 %conditional.11 = (bf16[64,4096]{1,0:T(8,128)(2,1)S(1)}, f32[4096]{0:T(1024)S(1)}) conditional(s32[]{:T(128)} %convert_element_type.706, () %tuple.336, (f32[2,4,64,64]{2,3,1,0:T(8,128)S(1)}, s32[]{:T(128)}, bf16[64,4096]{1,0:T(8,128)(2,1)S(1)}, bf16[1024,4096]{1,0:T(8,128)(2,1)}, bf16[2,64,1024]{2,1,0:T(8,128)(2,1)}, ...), branch_computations={%region_40.40_spmd, %region_41.45_spmd} | conditional | flops 2186538752 | bytes 48258384 | solution.py:248
  873.0 6.2 multiply_reduce_fusion.2
  882.2 6.3 reduce-scatter.9.cloned.1.call-done
  894.2 27.9 %conditional.11 = (bf16[64,4096]{1,0:T(8,128)(2,1)S(1)}, f32[4096]{0:T(1024)S(1)}) conditional(s32[]{:T(128)} %convert_element_type.706, () %tuple.336, (f32[2,4,64,64]{2,3,1,0:T(8,128)S(1)}, s32[]{:T(128)}, bf16[64,4096]{1,0:T(8,128)(2,1)S(1)}, bf16[1024,4096]{1,0:T(8,128)(2,1)}, bf16[2,64,1024]{2,1,0:T(8,128)(2,1)}, ...), branch_computations={%region_40.40_spmd, %region_41.45_spmd} | conditional | flops 2186538752 | bytes 48258384 | solution.py:248
  915.6 6.2 multiply_reduce_fusion.2
  924.7 6.6 reduce-scatter.9.cloned.1.call-done
  933.8 62.5 %all-reduce = (f32[1,4096]{1,0:T(1,128)}, f32[4096]{0:T(1024)}) all-reduce(f32[1,4096]{1,0:T(1,128)} %bitcast.442, f32[4096]{0:T(1024)S(1)} %get-tuple-element.2325), channel_id=1, replica_groups=mesh['dp'=8,'section'=2,'mp'=2] {'dp','mp'}, use_global_device_ids=true, to_apply=%region_48.49 | all-reduce | flops 8192 | bytes 65536 | tf_op jit(solution)/shard_map/psum | solution.py:291
  (285 shorter events, 227.5 us)
Async XLA Ops:
  7.2 509.8 %copy-start.13 = (f32[1,4096]{1,0:T(1,128)S(1)}, f32[1,4096]{1,0:T(1,128)}, u32[]{:S(2)}) copy-start(f32[1,4096]{1,0:T(1,128)} %param.65) | copy-start | bytes 49156
  7.2 130.6 %all-gather.19.cloned.1.call-start = ((), (), s32[]{:S(2)}) async-start(), calls=%async_computation.4 | async-start | bytes 9437184 | tf_op jit(solution)/shard_map/all_gather | solution.py:119
  7.9 255.2 %all-gather.21.cloned.1.call-start = ((), (), s32[]{:S(2)}) async-start(), calls=%async_computation.5 | async-start | bytes 9437184 | tf_op jit(solution)/shard_map/all_gather | solution.py:117
  8.7 379.7 %all-gather.23.cloned.1.call-start = ((), (), s32[]{:S(2)}) async-start(), calls=%async_computation.6 | async-start | bytes 9437184 | tf_op jit(solution)/shard_map/all_gather | solution.py:118
  9.4 504.5 %all-gather.25.cloned.1.call-start = ((), (), s32[]{:S(2)}) async-start(), calls=%async_computation.7 | async-start | bytes 9437184 | tf_op jit(solution)/shard_map/all_gather | solution.py:120
  517.0 36.0 %reduce-scatter.5.cloned.1.call-start = ((), (), s32[]{:S(2)}) async-start(), calls=%async_computation.11 | async-start | bytes 786432 | tf_op jit(solution)/shard_map/while/body/eval_jaxpr/reduce_scatter | solution.py:148
  555.3 35.9 %reduce-scatter.5.cloned.1.call-start = ((), (), s32[]{:S(2)}) async-start(), calls=%async_computation.11 | async-start | bytes 786432 | tf_op jit(solution)/shard_map/while/body/eval_jaxpr/reduce_scatter | solution.py:148
  593.5 29.6 %all-reduce.4.cloned.1.call-start = ((), (), s32[]{:S(2)}) async-start(), calls=%async_computation.8 | async-start | bytes 1048576 | tf_op jit(solution)/shard_map/psum | solution.py:14
  595.4 40.3 %all-gather.27.cloned.1.call-start = ((), (), s32[]{:S(2)}) async-start(), calls=%async_computation.9 | async-start | bytes 1572864 | tf_op jit(solution)/shard_map/all_gather | solution.py:197
  624.4 11.3 %copy-start.17 = (f32[2,32]{1,0:T(2,128)}, f32[2,32]{1,0:T(2,128)S(1)}, u32[]{:S(2)}) copy-start(f32[2,32]{1,0:T(2,128)S(1)} %add_sqrt_fusion.4) | copy-start | bytes 772
  635.7 33.1 %reduce-scatter.7.cloned.1.call-start = ((), (), s32[]{:S(2)}) async-start(), calls=%async_computation.12 | async-start | bytes 786432 | tf_op jit(solution)/shard_map/while/body/eval_jaxpr/reduce_scatter | solution.py:148
  671.2 36.3 %reduce-scatter.7.cloned.1.call-start = ((), (), s32[]{:S(2)}) async-start(), calls=%async_computation.12 | async-start | bytes 786432 | tf_op jit(solution)/shard_map/while/body/eval_jaxpr/reduce_scatter | solution.py:148
  712.2 45.0 %reduce-scatter.11.cloned.1.call-start = ((), (), s32[]{:S(2)}) async-start(), calls=%async_computation.14 | async-start | bytes 786432 | tf_op jit(solution)/shard_map/while/body/eval_jaxpr/reduce_scatter | solution.py:251
  759.6 41.8 %reduce-scatter.11.cloned.1.call-start = ((), (), s32[]{:S(2)}) async-start(), calls=%async_computation.14 | async-start | bytes 786432 | tf_op jit(solution)/shard_map/while/body/eval_jaxpr/reduce_scatter | solution.py:251
  803.9 40.6 %all-reduce.6.cloned.1.call-start = ((), (), s32[]{:S(2)}) async-start(), calls=%async_computation.10 | async-start | bytes 2097152 | tf_op jit(solution)/shard_map/psum | solution.py:278
  848.5 40.0 %reduce-scatter.9.cloned.1.call-start = ((), (), s32[]{:S(2)}) async-start(), calls=%async_computation.13 | async-start | bytes 786432 | tf_op jit(solution)/shard_map/while/body/eval_jaxpr/reduce_scatter | solution.py:251
  851.6 28.7 %copy-start.14 = (f32[4096]{0:T(1024)S(1)}, f32[4096]{0:T(1024)}, u32[]{:S(2)}) copy-start(f32[4096]{0:T(1024)} %get-tuple-element.3225) | copy-start | bytes 49156 | tf_op jit(solution)/shard_map/while
  851.6 28.8 %copy-start.16 = (s32[3]{0:T(128)S(1)}, s32[3]{0:T(128)}, u32[]{:S(2)}) copy-start(s32[3]{0:T(128)} %get-tuple-element.3263) | copy-start | bytes 40 | tf_op jit(solution)/shard_map/while
  851.6 7.3 copy-start.4
  880.4 10.6 %copy-start.15 = (f32[4096]{0:T(1024)}, f32[4096]{0:T(1024)S(1)}, u32[]{:S(2)}) copy-start(f32[4096]{0:T(1024)S(1)} %add.484) | copy-start | bytes 49156 | tf_op jit(solution)/shard_map/while
  891.0 40.2 %reduce-scatter.9.cloned.1.call-start = ((), (), s32[]{:S(2)}) async-start(), calls=%async_computation.13 | async-start | bytes 786432 | tf_op jit(solution)/shard_map/while/body/eval_jaxpr/reduce_scatter | solution.py:251
  894.2 28.7 %copy-start.14 = (f32[4096]{0:T(1024)S(1)}, f32[4096]{0:T(1024)}, u32[]{:S(2)}) copy-start(f32[4096]{0:T(1024)} %get-tuple-element.3225) | copy-start | bytes 49156 | tf_op jit(solution)/shard_map/while
  894.2 28.8 %copy-start.16 = (s32[3]{0:T(128)S(1)}, s32[3]{0:T(128)}, u32[]{:S(2)}) copy-start(s32[3]{0:T(128)} %get-tuple-element.3263) | copy-start | bytes 40 | tf_op jit(solution)/shard_map/while
  922.9 10.9 %copy-start.15 = (f32[4096]{0:T(1024)}, f32[4096]{0:T(1024)S(1)}, u32[]{:S(2)}) copy-start(f32[4096]{0:T(1024)S(1)} %add.484) | copy-start | bytes 49156 | tf_op jit(solution)/shard_map/while
  (21 other events, 80.6 us)
Sparse Core Ops, SparseCore 0:
  10.1 127.6 all-gather.18
  139.9 123.1 all-gather.20
  265.2 123.1 all-gather.22
  390.3 123.5 all-gather.24
  540.7 5.2 reduce-scatter.4
  579.0 5.2 reduce-scatter.4
  597.2 25.8 all-reduce.3
  626.6 9.0 all-gather.26
  640.2 28.5 reduce-scatter.6
  675.7 31.7 reduce-scatter.6
  717.0 40.0 reduce-scatter.10
  764.5 36.8 reduce-scatter.10
  807.2 37.2 all-reduce.5
  880.5 7.9 reduce-scatter.8
  923.0 8.1 reduce-scatter.8
where the time goes:
time: 1010 us; the launch traced here: 1000 us
  waiting for transfers between devices  694 us (69%)
  matrix products  87.8 us (9%)
  other arithmetic  81.2 us (8%)
  blocking collectives  79.9 us (8%)
  local copies, waits for them, and re-layouts  44.4 us (4%)
  between operations  13.9 us (1%)
    all_gather x1, waiting for transfers between devices, shards(): lax.all_gather(w_output, 'dp', axis=2, tiled=True)  126 us
    all_gather x1, waiting for transfers between devices, shards(): lax.all_gather(w_key, 'dp', axis=1, tiled=True)  125 us
    all_gather x1, waiting for transfers between devices, shards(): lax.all_gather(w_query, 'dp', axis=1, tiled=True)  125 us
    all_gather x1, waiting for transfers between devices, shards(): lax.all_gather(w_value, 'dp', axis=1, tiled=True)  124 us
    reduce_scatter x4, waiting for transfers between devices, backward_step(): lax.psum_scatter(grad_part.astype(jnp.bfloat16), 'mp', scatter_dimension=...  76.8 us
    psum x1, blocking collectives, shards(): gain_total = lax.psum(carry[2], ('dp', 'mp'))  62.5 us
    reduce_scatter x4, waiting for transfers between devices, layer_forward(): lax.psum_scatter(partial_value.astype(jnp.bfloat16), 'mp', scatter_dimens...  39.6 us
    psum x1, waiting for transfers between devices, shards(): lax.psum(carry[1].astype(jnp.bfloat16), ('section', 'mp'))  37.9 us
  transfers between devices with their start and end apart: 15, of which 13 were waited for; matrix products, arithmetic and copies ran while one was open for 7% of the time, Pallas kernels for 0%

commit v1 on v0

v1 whole, which is shorter than its diff:
```python
import jax
import jax.numpy as jnp
from jax import lax
from jax.sharding import PartitionSpec as P

HD = 256

epsilon = 1e-06


def gather_weights(wq, wk, wv, wo):
    return (
        lax.all_gather(wq, "dp", axis=0, tiled=True),
        lax.all_gather(wk, "dp", axis=0, tiled=True),
        lax.all_gather(wv, "dp", axis=0, tiled=True),
        lax.all_gather(wo, "dp", axis=1, tiled=True),
    )


def segment_ids(lengths, count):
    ends = jnp.cumsum(lengths, axis=-1)
    position = jnp.arange(count, dtype=jnp.int32)
    above = (position[None, :, None] >= ends[:, None, :-1]).astype(jnp.int32)
    return jnp.sum(above, axis=-1)


def rms_norm(inputs, norm_gain):
    floats = inputs.astype(jnp.float32)
    spread = jnp.sqrt(jnp.mean(floats * floats, axis=-1, keepdims=True) + epsilon)
    normal = floats / spread
    return (normal * norm_gain, normal, spread)


def norm_back(grad_out, normal, spread, norm_gain):
    scaled = grad_out * norm_gain
    return (scaled - normal * jnp.mean(scaled * normal, axis=-1, keepdims=True)) / spread


def dot(left, right):
    return jnp.dot(left, right, preferred_element_type=jnp.float32)


def dot_t(left, right):
    return lax.dot_general(left, right, (((1,), (1,)), ((), ())), preferred_element_type=jnp.float32)


def heads_of(rows, micro):
    return rows.reshape(micro, rows.shape[0] // micro, -1, HD)


def heads_einsum(spec, left, right):
    return jnp.einsum(spec, left, right, preferred_element_type=jnp.float32)


def softmax_scores(query, key, same_doc):
    scores = heads_einsum("mqhd,mkhd->mhqk", query, key) * HD ** (-0.5)
    scores = jnp.where(same_doc[:, None], scores, -1e30)
    exponent = jnp.exp(scores - jnp.max(scores, axis=-1, keepdims=True))
    return exponent / jnp.sum(exponent, axis=-1, keepdims=True)


def partner(array, axis):
    return lax.ppermute(array, axis, [(0, 1), (1, 0)])


def sum_of_all(array):
    array = array + partner(array, "mp")
    count = lax.axis_size("dp")
    step = 1
    while step < count:
        array = array + lax.ppermute(array, "dp", [(i, i ^ step) for i in range(count)])
        step *= 2
    return array


def shards(
    enc_input, dec_input, enc_lengths, dec_lengths, w_query, w_key, w_value, w_output,
    layer_gains, final_gain, cotangent,
):
    is_encoder = lax.axis_index("section") == 0
    core = lax.axis_index("mp")
    micro, piece, width = enc_input.shape[1:]
    count = piece * lax.axis_size("mp")
    rows = micro * count
    gain = layer_gains[0]

    def all_rows(pieces):
        return lax.all_gather(pieces, "mp", axis=1, tiled=True).reshape(rows, width)

    def add_pieces(partial_rows):
        halves = partial_rows.astype(jnp.bfloat16).reshape(micro, 2, piece, width)
        mine = lax.dynamic_index_in_dim(halves, core, 1, keepdims=False)
        other = lax.dynamic_index_in_dim(halves, 1 - core, 1, keepdims=False)
        return mine.astype(jnp.float32) + partner(other, "mp").astype(jnp.float32)

    enc_seg = segment_ids(enc_lengths[0], count)
    dec_seg = segment_ids(dec_lengths[0], count)
    query_seg = jnp.where(is_encoder, enc_seg, dec_seg)
    same_doc = query_seg[:, :, None] == enc_seg[:, None, :]
    entry = jnp.where(is_encoder, enc_input[0], dec_input[0])
    inputs = all_rows(entry)
    grad_last = all_rows(cotangent[0])
    full_q, full_k, full_v, full_o = gather_weights(
        w_query[0], w_key[0], w_value[0], w_output[0]
    )
    hidden_f, normal, spread = rms_norm(inputs, gain)
    hidden = hidden_f.astype(jnp.bfloat16)
    query = heads_of(dot(hidden, full_q).astype(jnp.bfloat16), micro)

    def forward(source):
        key = heads_of(dot(source, full_k).astype(jnp.bfloat16), micro)
        value = heads_of(dot(source, full_v).astype(jnp.bfloat16), micro)
        attention = softmax_scores(query, key, same_doc)
        mixed = heads_einsum("mhqk,mkhd->mqhd", attention.astype(jnp.bfloat16), value)
        part = dot(mixed.astype(jnp.bfloat16).reshape(rows, -1), full_o)
        result = (entry.astype(jnp.float32) + add_pieces(part)).astype(jnp.bfloat16)
        return result, key, value, attention

    enc_out = forward(hidden)[0]
    from_enc = lax.ppermute(enc_out, "section", [(0, 1)])
    encoded = jnp.where(is_encoder, enc_out, from_enc)
    normed, enc_normal, enc_spread = rms_norm(encoded, final_gain)
    source = jnp.where(is_encoder, hidden, all_rows(normed.astype(jnp.bfloat16)))
    layer_out, key, value, attention = forward(source)
    attention_b = attention.astype(jnp.bfloat16)

    def score_grads(grad_rows):
        grad_mixed = heads_of(dot_t(grad_rows, full_o).astype(jnp.bfloat16), micro)
        grad_value = heads_einsum("mhqk,mqhd->mkhd", attention_b, grad_mixed)
        grad_att = heads_einsum("mqhd,mkhd->mhqk", grad_mixed, value)
        shared = jnp.sum(attention * grad_att, axis=-1, keepdims=True)
        grad_scores = (attention * (grad_att - shared) * HD ** (-0.5)).astype(jnp.bfloat16)
        grad_key = heads_einsum("mhqk,mqhd->mkhd", grad_scores, query)
        grad_source = dot_t(grad_key.astype(jnp.bfloat16).reshape(rows, -1), full_k)
        grad_source = grad_source + dot_t(
            grad_value.astype(jnp.bfloat16).reshape(rows, -1), full_v
        )
        return grad_scores, grad_source

    cross = add_pieces(score_grads(grad_last)[1])
    cross_sent = lax.ppermute(cross.astype(jnp.bfloat16), "section", [(1, 0)])
    cross = jnp.where(is_encoder, cross_sent, cross.astype(jnp.bfloat16)).astype(jnp.float32)
    enc_grads = norm_back(cross, enc_normal, enc_spread, final_gain).astype(jnp.bfloat16)
    final_part = jnp.sum(cross * enc_normal, axis=(0, 1))

    grad_piece = jnp.where(is_encoder, enc_grads, cotangent[0])
    grad_rows = all_rows(grad_piece)
    grad_scores, grad_source = score_grads(grad_rows)
    grad_query = heads_einsum("mhqk,mkhd->mqhd", grad_scores, key)
    grad_hidden = dot_t(grad_query.astype(jnp.bfloat16).reshape(rows, -1), full_q)
    grad_hidden = grad_hidden + jnp.where(is_encoder, grad_source, 0.0)
    grad_part = norm_back(grad_hidden, normal, spread, gain)
    gain_part = jnp.sum(grad_hidden * normal, axis=0)
    totals = sum_of_all(jnp.stack([gain_part, final_part]))
    input_grad = (grad_piece.astype(jnp.float32) + add_pieces(grad_part)).astype(jnp.bfloat16)
    return (layer_out[None, None], input_grad[None, None], totals[:1], totals[1])


def solution(mesh):
    return jax.shard_map(
        shards,
        mesh=mesh,
        in_specs=(
            P("dp", None, "mp", None),
            P("dp", None, "mp", None),
            P("dp", None, None),
            P("dp", None, None),
            P("section", "dp", "mp"),
            P("section", "dp", "mp"),
            P("section", "dp", "mp"),
            P("section", "mp", "dp"),
            P("section", None),
            P(),
            P("dp", None, "mp", None),
        ),
        out_specs=(
            P("section", "dp", None, "mp", None),
            P("section", "dp", None, "mp", None),
            P("section", None),
            P(),
        ),
        check_vma=False,
    )
```

time: 1010 us -> 677 us (0.67)
  waiting for transfers between devices: 694 us -> 536 us
  blocking collectives: 79.9 us -> 0 us
  other arithmetic: 81.2 us -> 13.7 us
  local copies, waits for them, and re-layouts: 44.4 us -> 10.5 us
  starting transfers between devices: 0.44 us -> 12.7 us
    reduce_scatter x8 -> x0, waiting for transfers between devices: 116 us -> none  [the longest x4 76.8 us: backward_step(): lax.psum_scatter(grad_part.astype(jnp.bfloat16), 'mp', scatter_dimension=...]
    psum x2 -> x0, waiting for transfers between devices: 65.4 us -> none  [the longest x1 37.9 us: shards(): lax.psum(carry[1].astype(jnp.bfloat16), ('section', 'mp'))]
    psum x1 -> x0, blocking collectives: 62.5 us -> none  [shards(): gain_total = lax.psum(carry[2], ('dp', 'mp'))]
    scatter x24 -> x0, other arithmetic: 38.9 us -> none  [the longest x20 28.8 us: keep(): return table.at[slot].set(jnp.where(is_valid, value, table[slot]))]
    ppermute x0 -> x10, waiting for transfers between devices: none -> 34.9 us  [the longest x1 14.4 us: shards(): cross_sent = lax.ppermute(cross.astype(jnp.bfloat16), 'section', [(1, 0)])]
    dynamic_slice x40 -> x0, local copies, waits for them, and re-layouts: 26.8 us -> none  [the longest x24 15.2 us: keep(): return table.at[slot].set(jnp.where(is_valid, value, table[slot]))]
    all_gather x8 -> x0, blocking collectives: 17.5 us -> none  [the longest x4 8.73 us: layer_forward(): inputs = lax.all_gather(inputs_piece, 'mp', axis=0, tiled=True)]
    another operation x12 -> x1, other arithmetic: 15.3 us -> 0.04 us  [shards(): totals = sum_of_all(jnp.stack([gain_part, final_part]))]
  transfers between devices with their start and end apart: 15 -> 18, of which waited for: 13 -> 14; matrix products, arithmetic and copies ran while one was open for 7% -> 10% of each run, Pallas kernels for 0% -> 0%
where the time goes in v1:
time: 677 us; the launch traced here: 676 us
  waiting for transfers between devices  536 us (79%)
  matrix products  88.7 us (13%)
  between operations  14.7 us (2%)
  other arithmetic  13.7 us (2%)
  starting transfers between devices  12.7 us (2%)
  local copies, waits for them, and re-layouts  10.5 us (2%)
    all_gather x1, waiting for transfers between devices, gather_weights(): lax.all_gather(wk, 'dp', axis=0, tiled=True)  125 us
    all_gather x1, waiting for transfers between devices, gather_weights(): lax.all_gather(wq, 'dp', axis=0, tiled=True)  120 us
    all_gather x1, waiting for transfers between devices, gather_weights(): lax.all_gather(wv, 'dp', axis=0, tiled=True)  120 us
    all_gather x1, waiting for transfers between devices, gather_weights(): lax.all_gather(wo, 'dp', axis=1, tiled=True)  120 us
    dot_general x7, matrix products, dot_t(): lax.dot_general(left, right, (((1,), (1,)), ((), ())), preferred_element_...  41.8 us
    dot_general x7, matrix products, dot(): return jnp.dot(left, right, preferred_element_type=jnp.float32)  33.9 us
    ppermute x1, waiting for transfers between devices, shards(): cross_sent = lax.ppermute(cross.astype(jnp.bfloat16), 'section', [(1, 0)])  14.4 us
  transfers between devices with their start and end apart: 18, of which 14 were waited for; matrix products, arithmetic and copies ran while one was open for 10% of the time, Pallas kernels for 0%

profile of v1, /device:TPU:0, one launch (start us, length us, event | category | flops | bytes accessed | tf_op | source)
XLA Modules:
  0.0 676.2 jit_solution(6751112088220566714)
XLA Ops:
  12.5 9.4 %all-gather.19.cloned.1.call-done = bf16[1,2,64,4096]{3,2,1,0:T(8,128)(2,1)} async-done(((bf16[1,2,32,4096]{3,2,1,0:T(8,128)(2,1)}), bf16[1,2,64,4096]{3,2,1,0:T(8,128)(2,1)}) %all-gather.19.cloned.1.call-update) | async-done | bytes 1048592 | tf_op jit(solution)/shard_map/all_gather | solution.py:88
  25.1 125.1 %all-gather.25.cloned.1.call-done = bf16[1,4096,1024]{2,1,0:T(8,128)(2,1)} async-done(((bf16[1,512,1024]{2,1,0:T(8,128)(2,1)}), bf16[1,4096,1024]{2,1,0:T(8,128)(2,1)}) %all-gather.25.cloned.1.call-update) | async-done | bytes 8388624 | tf_op jit(solution)/shard_map/all_gather | solution.py:14
  150.1 4.6 fusion.66
  155.0 120.5 %all-gather.23.cloned.1.call-done = bf16[1,4096,1024]{2,1,0:T(8,128)(2,1)} async-done(((bf16[1,512,1024]{2,1,0:T(8,128)(2,1)}), bf16[1,4096,1024]{2,1,0:T(8,128)(2,1)}) %all-gather.23.cloned.1.call-update) | async-done | bytes 8388624 | tf_op jit(solution)/shard_map/all_gather | solution.py:13
  275.4 4.6 fusion.63
  280.3 120.3 %all-gather.21.cloned.1.call-done = bf16[1,4096,1024]{2,1,0:T(8,128)(2,1)} async-done(((bf16[1,512,1024]{2,1,0:T(8,128)(2,1)}), bf16[1,4096,1024]{2,1,0:T(8,128)(2,1)}) %all-gather.21.cloned.1.call-update) | async-done | bytes 8388624 | tf_op jit(solution)/shard_map/all_gather | solution.py:15
  400.6 4.6 fusion.57
  406.3 119.8 %all-gather.27.cloned.1.call-done = bf16[1,1024,4096]{2,1,0:T(8,128)(2,1)} async-done(((bf16[1,1024,512]{2,1,0:T(8,128)(2,1)}), bf16[1,1024,4096]{2,1,0:T(8,128)(2,1)}) %all-gather.27.cloned.1.call-update) | async-done | bytes 8388624 | tf_op jit(solution)/shard_map/all_gather | solution.py:16
  526.1 4.7 fusion.44
  533.0 3.4 collective-permute-start.1
  536.5 11.4 %collective-permute-done.1 = bf16[2,32,4096]{2,1,0:T(8,128)(2,1)S(1)} collective-permute-done((bf16[2,32,4096]{2,1,0:T(8,128)(2,1)S(1)}, bf16[2,32,4096]{2,1,0:T(8,128)(2,1)S(1)}, u32[]{:S(2)}, u32[]{:S(2)}) %collective-permute-start.1) | collective-permute-done | bytes 524320 | tf_op jit(solution)/shard_map/ppermute | solution.py:120
  549.4 6.7 fusion.72
  559.2 5.3 fusion.60
  565.7 5.3 fusion.69
  580.0 6.2 fusion.14
  586.2 6.3 fusion.41
  596.1 14.4 %collective-permute-done.4 = bf16[2,32,4096]{2,1,0:T(8,128)(2,1)S(1)} collective-permute-done((bf16[2,32,4096]{2,1,0:T(8,128)(2,1)S(1)}, bf16[2,32,4096]{2,1,0:T(8,128)(2,1)S(1)}, u32[]{:S(2)}, u32[]{:S(2)}) %collective-permute-start.4) | collective-permute-done | bytes 524320 | tf_op jit(solution)/shard_map/ppermute | solution.py:141
  613.9 4.6 fusion.47
  619.4 2.8 all-gather.17.cloned.1.call-done
  622.2 6.6 fusion.75
  637.4 6.4 fusion.12
  643.8 6.4 fusion.50
  650.2 3.2 multiply_reduce_fusion.1
  662.8 2.8 collective-permute-start.9
  (141 shorter events, 55.9 us)
Async XLA Ops:
  7.2 14.7 %all-gather.19.cloned.1.call-start = ((), (), s32[]{:S(2)}) async-start(), calls=%async_computation.2 | async-start | bytes 1572864 | tf_op jit(solution)/shard_map/all_gather | solution.py:88
  9.2 141.0 %all-gather.25.cloned.1.call-start = ((), (), s32[]{:S(2)}) async-start(), calls=%async_computation.5 | async-start | bytes 9437184 | tf_op jit(solution)/shard_map/all_gather | solution.py:14
  9.9 13.6 %copy-start.14 = (f32[1,4096]{1,0:T(1,128)S(1)}, f32[1,4096]{1,0:T(1,128)}, u32[]{:S(2)}) copy-start(f32[1,4096]{1,0:T(1,128)} %param.19) | copy-start | bytes 49156
  9.9 265.5 %all-gather.23.cloned.1.call-start = ((), (), s32[]{:S(2)}) async-start(), calls=%async_computation.4 | async-start | bytes 9437184 | tf_op jit(solution)/shard_map/all_gather | solution.py:13
  10.7 389.9 %all-gather.21.cloned.1.call-start = ((), (), s32[]{:S(2)}) async-start(), calls=%async_computation.3 | async-start | bytes 9437184 | tf_op jit(solution)/shard_map/all_gather | solution.py:15
  11.2 514.8 %all-gather.27.cloned.1.call-start = ((), (), s32[]{:S(2)}) async-start(), calls=%async_computation.6 | async-start | bytes 9437184 | tf_op jit(solution)/shard_map/all_gather | solution.py:16
  11.8 537.6 %all-gather.29.cloned.1.call-start = ((), (), s32[]{:S(2)}) async-start(), calls=%async_computation.7 | async-start | bytes 1572864 | tf_op jit(solution)/shard_map/all_gather | solution.py:88
  280.3 125.1 %copy-start.6 = (bf16[2,64,4,256]{3,2,1,0:T(4,128)(2,1)}, bf16[2,64,4,256]{3,2,1,0:T(4,128)(2,1)S(1)}, u32[]{:S(2)}) copy-start(bf16[2,64,4,256]{3,2,1,0:T(4,128)(2,1)S(1)} %reshape.134) | copy-start | bytes 786436
  530.8 17.3 %copy-start.13 = (f32[4096]{0:T(1024)S(1)}, f32[4096]{0:T(1024)}, u32[]{:S(2)}) copy-start(f32[4096]{0:T(1024)} %param.20) | copy-start | bytes 49156
  530.8 2.0 collective-permute-start
  533.0 14.8 %collective-permute-start.1 = (bf16[2,32,4096]{2,1,0:T(8,128)(2,1)S(1)}, bf16[2,32,4096]{2,1,0:T(8,128)(2,1)S(1)}, u32[]{:S(2)}, u32[]{:S(2)}) collective-permute-start(bf16[2,32,4096]{2,1,0:T(8,128)(2,1)S(1)} %fusion.102), channel_id=1, source_target_pairs={{0,2},{1,3},{4,6},{5,7},{8,10},{9,11},{12,14},{13,15},{16,18},{17,... | collective-permute-start | bytes 1572872 | tf_op jit(solution)/shard_map/ppermute | solution.py:120
  536.5 21.1 %all-gather.15.cloned.1.call-start = ((), (), s32[]{:S(2)}) async-start(), calls=%async_computation | async-start | bytes 1572864 | tf_op jit(solution)/shard_map/all_gather | solution.py:88
  549.2 73.0 %all-gather.17.cloned.1.call-start = ((), (), s32[]{:S(2)}) async-start(), calls=%async_computation.1 | async-start | bytes 1572864 | tf_op jit(solution)/shard_map/all_gather | solution.py:88
  549.4 8.1 %copy-start = (bf16[1,2,64,4096]{3,2,1,0:T(8,128)(2,1)S(1)}, bf16[1,2,64,4096]{3,2,1,0:T(8,128)(2,1)}, u32[]{:S(2)}) copy-start(bf16[1,2,64,4096]{3,2,1,0:T(8,128)(2,1)} %all-gather.19.cloned.1.call-done) | copy-start | bytes 3145732
  592.5 18.5 %copy-start.4 = (bf16[1,2,32,4096]{3,2,1,0:T(8,128)(2,1)S(1)}, bf16[1,2,32,4096]{3,2,1,0:T(8,128)(2,1)}, u32[]{:S(2)}) copy-start(bf16[1,2,32,4096]{3,2,1,0:T(8,128)(2,1)} %param.21) | copy-start | bytes 1572868
  592.5 2.0 collective-permute-start.3
  594.6 15.9 %collective-permute-start.4 = (bf16[2,32,4096]{2,1,0:T(8,128)(2,1)S(1)}, bf16[2,32,4096]{2,1,0:T(8,128)(2,1)S(1)}, u32[]{:S(2)}, u32[]{:S(2)}) collective-permute-start(bf16[2,32,4096]{2,1,0:T(8,128)(2,1)S(1)} %fusion.106), channel_id=1, source_target_pairs={{2,0},{3,1},{6,4},{7,5},{10,8},{11,9},{14,12},{15,13},{18,16},{19,... | collective-permute-start | bytes 1572872 | tf_op jit(solution)/shard_map/ppermute | solution.py:141
  619.4 34.3 %collective-permute-start.2 = (bf16[2,32,4096]{2,1,0:T(8,128)(2,1)}, bf16[2,32,4096]{2,1,0:T(8,128)(2,1)S(1)}, u32[]{:S(2)}, u32[]{:S(2)}) collective-permute-start(bf16[2,32,4096]{2,1,0:T(8,128)(2,1)} %dynamic-slice_bitcast_fusion.2), channel_id=1, source_target_pairs={{0,1},{1,0},{2,3},{3,2},{4,5},{5,4},{6,7},{7,6},{8,9},{9,8},{10,11... | collective-permute-start | bytes 1572872 | tf_op jit(solution)/shard_map/ppermute | solution.py:63
  637.3 12.8 %slice-start = ((s8[8388608]{0:T(1024)(128)(4,1)}), s8[4194304]{0:T(1024)(128)(4,1)S(1)}, s32[]{:S(2)}) async-start(s8[8388608]{0:T(1024)(128)(4,1)} %bitcast.183), calls=%async_computation.8 | async-start | bytes 8388608
  653.4 1.3 collective-permute-start.6
  654.8 4.0 collective-permute-start.7
  658.8 4.0 collective-permute-start.8
  662.8 4.9 collective-permute-start.9
  665.7 2.7 collective-permute-start.5
  (13 other events, 53.9 us)
Sparse Core Ops, SparseCore 0:
  10.1 11.7 all-gather.18
  24.0 126.0 all-gather.24
  152.3 123.1 all-gather.22
  277.4 123.1 all-gather.20
  402.5 123.5 all-gather.26
  536.6 6.2 all-gather.28
  549.3 8.2 all-gather.14
  612.4 9.7 all-gather.16

commit v2 on v1

--- a/solution.py
+++ b/solution.py
@@ -1,20 +1,209 @@
+import functools
+
 import jax
 import jax.numpy as jnp
 from jax import lax
+from jax.experimental import pallas as pl
+from jax.experimental.pallas import tpu as pltpu
 from jax.sharding import PartitionSpec as P
 
 HD = 256
+MESH = pl.DeviceIdType.MESH
 
 epsilon = 1e-06
 
 
+def gather_kernel(
+    lines, parts, crossed, wq, wk, wv, wo, oq, ok, ov, oo,
+    send_right, send_left, recv_z, send_y, recv_y, local_sem,
+):
+    me = lax.axis_index("dp")
+    a = me // 2
+    b = me % 2
+    ins = (wq, wk, wv, wo)
+    outs = (oq, ok, ov, oo)
+
+    def own(w, p):
+        size = ins[w].shape[0] // parts
+        return ins[w].at[pl.ds(pl.multiple_of(p * size, size), size), :]
+
+    def slot(w, line, side, p):
+        size = ins[w].shape[0] // parts
+        block = line * 2 + side
+        if w < 3:
+            start = block * ins[w].shape[0] + p * size
+            return outs[w].at[pl.ds(pl.multiple_of(start, size), size), :]
+        cols = ins[w].shape[1]
+        return outs[w].at[
+            pl.ds(pl.multiple_of(p * size, size), size),
+            pl.ds(pl.multiple_of(block * cols, cols), cols),
+        ]
+
+    def along(w, p, line, side, right, src=None):
+        dst = slot(w, line, side, p)
+        sem = (send_right if right else send_left).at[side, w * parts + p, line]
+        target = (a + 1) if right else (a - 1)
+        return pltpu.make_async_remote_copy(
+            src_ref=dst if src is None else src, dst_ref=dst, send_sem=sem,
+            recv_sem=recv_z.at[side, w * parts + p, line],
+            device_id={"dp": target * 2 + b}, device_id_type=MESH,
+        )
+
+    def across(w, p, line, side, src=None):
+        dst = slot(w, line, side, p)
+        return pltpu.make_async_remote_copy(
+            src_ref=dst if src is None else src, dst_ref=dst,
+            send_sem=send_y.at[w * parts + p, line],
+            recv_sem=recv_y.at[w * parts + p, line],
+            device_id={"dp": a * 2 + 1 - b}, device_id_type=MESH,
+        )
+
+    def each(first, last, w, body):
+        if last[w] > first[w]:
+            lax.fori_loop(first[w], last[w], lambda p, c: (body(p), c)[1], 0)
+
+    none = [0] * 4
+    split = [parts - crossed[w] for w in range(4)]
+    full = [parts] * 4
+    has_right = a + 1 < lines
+    has_left = a > 0
+
+    barrier = pltpu.get_barrier_semaphore()
+    pl.semaphore_signal(barrier, inc=1, device_id={"dp": a * 2 + 1 - b}, device_id_type=MESH)
+
+    @pl.when(has_right)
+    def _():
+        pl.semaphore_signal(barrier, inc=1, device_id={"dp": me + 2}, device_id_type=MESH)
+
+    @pl.when(has_left)
+    def _():
+        pl.semaphore_signal(barrier, inc=1, device_id={"dp": me - 2}, device_id_type=MESH)
+
+    peers = 1 + has_right.astype(jnp.int32) + has_left.astype(jnp.int32)
+    pl.semaphore_wait(barrier, peers)
+
+    def both_ways(w, p, line, side, src, op):
+        @pl.when(has_right)
+        def _():
+            op(along(w, p, line, side, True, src))
+
+        @pl.when(has_left)
+        def _():
+            op(along(w, p, line, side, False, src))
+
+    def start(copy):
+        copy.start()
+
+    def sent(copy):
+        copy.wait_send()
+
+    def begin(w, p):
+        across(w, p, a, b, own(w, p)).start()
+        both_ways(w, p, a, b, own(w, p), start)
+
+    for w in range(4):
+        each(split, full, w, functools.partial(begin, w))
+    for w in range(4):
+        each(none, split, w, functools.partial(begin, w))
+    for w in range(4):
+        each(none, full, w, lambda p, w=w: pltpu.make_async_copy(
+            own(w, p), slot(w, a, b, p), local_sem.at[w * parts + p]).start())
+
+    def turn(w, p):
+        across(w, p, a, 1 - b).wait_recv()
+        both_ways(w, p, a, 1 - b, None, start)
+
+    for w in range(4):
+        each(split, full, w, functools.partial(turn, w))
+
+    def relay(w, p, dist, side, cross, op):
+        @pl.when(a - dist >= 0)
+        def _():
+            line = a - dist
+            if op is start:
+                along(w, p, line, side, True).wait_recv()
+
+            @pl.when(has_right)
+            def _():
+                op(along(w, p, line, side, True))
+
+            if cross:
+                op(across(w, p, line, side))
+
+        @pl.when(a + dist < lines)
+        def _():
+            line = a + dist
+            if op is start:
+                along(w, p, line, side, False).wait_recv()
+
+            @pl.when(has_left)
+            def _():
+                op(along(w, p, line, side, False))
+
+            if cross:
+                op(across(w, p, line, side))
+
+    def hop(dist, op):
+        for w in range(4):
+            def crossed_part(p, w=w):
+                relay(w, p, dist, b, False, op)
+                relay(w, p, dist, 1 - b, False, op)
+
+            each(split, full, w, crossed_part)
+            each(none, split, w, lambda p, w=w: relay(w, p, dist, b, True, op))
+
+    def hop_start(dist, c):
+        hop(dist, start)
+        return c
+
+    def hop_sent(dist, c):
+        hop(dist, sent)
+        return c
+
+    lax.fori_loop(1, lines, hop_start, 0)
+    for w in range(4):
+        def arrived(p, w=w):
+            def one(line, c):
+                across(w, p, line, 1 - b).wait_recv()
+                return c
+
+            lax.fori_loop(0, lines, one, 0)
+
+        each(none, split, w, arrived)
+
+    for w in range(4):
+        def finish(p, w=w):
+            across(w, p, a, b, own(w, p)).wait_send()
+            both_ways(w, p, a, b, own(w, p), sent)
+            pltpu.make_async_copy(
+                own(w, p), slot(w, a, b, p), local_sem.at[w * parts + p]).wait()
+
+        each(none, full, w, finish)
+        each(split, full, w, lambda p, w=w: both_ways(w, p, a, 1 - b, None, sent))
+    lax.fori_loop(1, lines, hop_sent, 0)
+
+
 def gather_weights(wq, wk, wv, wo):
-    return (
-        lax.all_gather(wq, "dp", axis=0, tiled=True),
-        lax.all_gather(wk, "dp", axis=0, tiled=True),
-        lax.all_gather(wv, "dp", axis=0, tiled=True),
-        lax.all_gather(wo, "dp", axis=1, tiled=True),
-    )
+    count = lax.axis_size("dp")
+    lines = count // 2
+    parts = max(1, 16 // lines)
+    crossed = (1, 1, 1, 0) if parts > 1 else (0, 0, 0, 0)
+    units = 4 * parts
+    rows, width = wq.shape
+    tall = jax.ShapeDtypeStruct((rows * count, width), wq.dtype)
+    wide = jax.ShapeDtypeStruct((wo.shape[0], wo.shape[1] * count), wo.dtype)
+    dma = pltpu.SemaphoreType.DMA
+    return pl.pallas_call(
+        functools.partial(gather_kernel, lines, parts, crossed),
+        out_shape=(tall, tall, tall, wide),
+        in_specs=[pl.BlockSpec(memory_space=pl.ANY)] * 4,
+        out_specs=[pl.BlockSpec(memory_space=pl.ANY)] * 4,
+        scratch_shapes=[
+            dma((2, units, lines)), dma((2, units, lines)), dma((2, units, lines)),
+            dma((units, lines)), dma((units, lines)), dma((units,)),
+        ],
+        compiler_params=pltpu.CompilerParams(collective_id=0, has_side_effects=True),
+    )(wq, wk, wv, wo)
 
 
 def segment_ids(lengths, count):

time: 677 us -> 515 us (0.76)
  waiting for transfers between devices: 536 us -> 39.7 us
  Pallas kernels: 0 us -> 339 us
    all_gather x4 -> x0, waiting for transfers between devices: 486 us -> none  [the longest x1 125 us: gather_weights(): lax.all_gather(wk, 'dp', axis=0, tiled=True)]
    pallas_call x0 -> x1, Pallas kernels: none -> 339 us  [gather_weights(): pl.pallas_call(functools.partial(gather_kernel, lines, parts, crossed), o...]
    all_gather x4, waiting for transfers between devices: 12.7 us -> 4.71 us  [all_rows(): return lax.all_gather(pieces, 'mp', axis=1, tiled=True).reshape(rows, width)]
  transfers between devices with their start and end apart: 18 -> 14, of which waited for: 14 -> 9; matrix products, arithmetic and copies ran while one was open for 10% -> 10% of each run, Pallas kernels for 0% -> 66%
where the time goes in v2:
time: 515 us; the launch traced here: 514 us
  Pallas kernels  339 us (66%)
  matrix products  83.8 us (16%)
  waiting for transfers between devices  39.7 us (8%)
  other arithmetic  15.3 us (3%)
  between operations  14.4 us (3%)
  starting transfers between devices  12.6 us (2%)
  local copies, waits for them, and re-layouts  10 us (2%)
    pallas_call x1, Pallas kernels, gather_weights(): pl.pallas_call(functools.partial(gather_kernel, lines, parts, crossed), o...  339 us
    dot_general x7, matrix products, dot_t(): lax.dot_general(left, right, (((1,), (1,)), ((), ())), preferred_element_...  41.3 us
    dot_general x7, matrix products, dot(): return jnp.dot(left, right, preferred_element_type=jnp.float32)  29.5 us
    ppermute x1, waiting for transfers between devices, shards(): cross_sent = lax.ppermute(cross.astype(jnp.bfloat16), 'section', [(1, 0)])  14.4 us
    dot_general x11, matrix products, heads_einsum(): return jnp.einsum(spec, left, right, preferred_element_type=jnp.float32)  13 us
    ppermute x1, waiting for transfers between devices, shards(): from_enc = lax.ppermute(enc_out, 'section', [(0, 1)])  11.4 us
  transfers between devices with their start and end apart: 14, of which 9 were waited for; matrix products, arithmetic and copies ran while one was open for 10% of the time, Pallas kernels for 66%

profile of v2, /device:TPU:0, one launch (start us, length us, event | category | flops | bytes accessed | tf_op | source)
XLA Modules:
  0.0 514.4 jit_solution(17876124142576092778)
XLA Ops:
  9.6 338.6 %shard_map.138 = (bf16[4096,1024]{1,0:T(8,128)(2,1)}, bf16[4096,1024]{1,0:T(8,128)(2,1)}, bf16[4096,1024]{1,0:T(8,128)(2,1)}, bf16[1024,4096]{1,0:T(8,128)(2,1)}) custom-call(bf16[512,1024]{1,0:T(8,128)(2,1)} %bitcast.168, bf16[512,1024]{1,0:T(8,128)(2,1)} %bitcast.169, bf16[512,1024]{1,0:T(8,128)(2,1)} %bitcast.170, bf16[1024,512]{1,0:T(8,128)(2,1)} %bitcast.171), custom_call_target="tpu_custom_call" | custom-call | tf_op jit(solution)/shard_map/pallas_call | solution.py:196
  351.7 4.6 convolution_convert_fusion.14
  356.5 4.7 convolution_convert_fusion.15
  361.3 4.6 convolution_convert_fusion.13
  367.2 4.7 convolution_convert_fusion.1
  374.1 3.4 collective-permute-start.1
  377.6 11.4 %collective-permute-done.1 = bf16[2,32,4096]{2,1,0:T(8,128)(2,1)S(1)} collective-permute-done((bf16[2,32,4096]{2,1,0:T(8,128)(2,1)S(1)}, bf16[2,32,4096]{2,1,0:T(8,128)(2,1)S(1)}, u32[]{:S(2)}, u32[]{:S(2)}) %collective-permute-start.1) | collective-permute-done | bytes 524320 | tf_op jit(solution)/shard_map/ppermute | solution.py:309
  390.5 5.9 %fusion.28 = bf16[128,1024]{0,1:T(8,128)(2,1)S(1)} fusion(bf16[1024,4096]{1,0:T(8,128)(2,1)} %get-tuple-element.11, bf16[128,4096]{1,0:T(8,128)(2,1)} %bitcast.191), kind=kOutput, calls=%fused_computation.60 | convolution fusion | flops 1073872896 | bytes 9699328 | tf_op jit(solution)/shard_map/dot_general | solution.py:233
  401.5 4.9 convolution_convert_fusion.10
  413.7 2.1 fusion.14
  417.3 6.2 %fusion.84 = f32[128,4096]{1,0:T(8,128)S(1)} fusion(bf16[128,1024]{1,0:T(8,128)(2,1)S(1)} %bitcast.172, bf16[4096,1024]{1,0:T(8,128)(2,1)} %get-tuple-element.10), kind=kOutput, calls=%fused_computation.140 | convolution fusion | flops 1073741824 | bytes 10747904 | tf_op jit(solution)/shard_map/dot_general | solution.py:233
  423.5 6.3 %fusion.6 = bf16[128,4096]{1,0:T(8,128)(2,1)S(1)} fusion(f32[128,4096]{1,0:T(8,128)S(1)} %fusion.84, bf16[128,1024]{1,0:T(8,128)(2,1)S(1)} %bitcast.160, bf16[4096,1024]{1,0:T(8,128)(2,1)} %get-tuple-element.8), kind=kOutput, calls=%fused_computation.8 | convolution fusion | flops 1074790400 | bytes 11796480 | tf_op jit(solution)/shard_map/dot_general | solution.py:233
  433.5 14.4 %collective-permute-done.4 = bf16[2,32,4096]{2,1,0:T(8,128)(2,1)S(1)} collective-permute-done((bf16[2,32,4096]{2,1,0:T(8,128)(2,1)S(1)}, bf16[2,32,4096]{2,1,0:T(8,128)(2,1)S(1)}, u32[]{:S(2)}, u32[]{:S(2)}) %collective-permute-start.4) | collective-permute-done | bytes 524320 | tf_op jit(solution)/shard_map/ppermute | solution.py:330
  451.2 4.7 convolution_convert_fusion
  456.7 2.8 all-gather.9.cloned.1.call-done
  459.5 6.6 %convolution_convert_fusion.7 = bf16[128,1024]{1,0:T(8,128)(2,1)S(1)} fusion(bf16[128,4096]{1,0:T(8,128)(2,1)} %bitcast.159, bf16[1024,4096]{1,0:T(8,128)(2,1)} %get-tuple-element.11), kind=kOutput, calls=%fused_computation.32 | convolution fusion | flops 1073872896 | bytes 9699328 | tf_op jit(solution)/shard_map/dot_general | solution.py:233
  466.6 2.0 fusion.17
  470.0 2.0 fusion.16
  474.4 6.4 %fusion.86 = f32[128,4096]{1,0:T(8,128)S(1)} fusion(bf16[128,1024]{1,0:T(8,128)(2,1)S(1)} %bitcast.173, bf16[4096,1024]{1,0:T(8,128)(2,1)} %get-tuple-element.10), kind=kOutput, calls=%fused_computation.142 | convolution fusion | flops 1073741824 | bytes 10747904 | tf_op jit(solution)/shard_map/dot_general | solution.py:233
  481.1 6.4 %fusion.85 = f32[128,4096]{1,0:T(8,128)S(1)} fusion(bf16[128,1024]{1,0:T(8,128)(2,1)S(1)} %bitcast.174, bf16[4096,1024]{1,0:T(8,128)(2,1)} %get-tuple-element.9), kind=kOutput, calls=%fused_computation.141 | convolution fusion | flops 1073741824 | bytes 10747904 | tf_op jit(solution)/shard_map/dot_general | solution.py:233
  487.5 3.4 multiply_reduce_fusion.1
  491.3 2.0 fusion.42
  495.2 2.1 collective-permute-done.7
  501.4 2.8 collective-permute-start.9
  (128 shorter events, 46.9 us)
Async XLA Ops:
  7.2 341.3 %all-gather.11.cloned.1.call-start = ((), (), s32[]{:S(2)}) async-start(), calls=%async_computation.2 | async-start | bytes 1572864 | tf_op jit(solution)/shard_map/all_gather | solution.py:277
  9.2 381.4 %all-gather.13.cloned.1.call-start = ((), (), s32[]{:S(2)}) async-start(), calls=%async_computation.3 | async-start | bytes 1572864 | tf_op jit(solution)/shard_map/all_gather | solution.py:277
  9.6 340.5 %copy-start.10 = (f32[1,4096]{1,0:T(1,128)S(1)}, f32[1,4096]{1,0:T(1,128)}, u32[]{:S(2)}) copy-start(f32[1,4096]{1,0:T(1,128)} %param.19) | copy-start | bytes 49156
  356.5 9.8 %copy-start.5 = (bf16[2,64,4,256]{3,2,1,0:T(4,128)(2,1)}, bf16[2,64,4,256]{3,2,1,0:T(4,128)(2,1)S(1)}, u32[]{:S(2)}) copy-start(bf16[2,64,4,256]{3,2,1,0:T(4,128)(2,1)S(1)} %reshape.134) | copy-start | bytes 786436
  367.1 6.8 %copy-start.1 = (bf16[1,2,32,4096]{3,2,1,0:T(8,128)(2,1)S(1)}, bf16[1,2,32,4096]{3,2,1,0:T(8,128)(2,1)}, u32[]{:S(2)}) copy-start(bf16[1,2,32,4096]{3,2,1,0:T(8,128)(2,1)} %broadcast_select_fusion.2) | copy-start | bytes 1572868
  371.9 17.3 %copy-start.9 = (f32[4096]{0:T(1024)S(1)}, f32[4096]{0:T(1024)}, u32[]{:S(2)}) copy-start(f32[4096]{0:T(1024)} %param.20) | copy-start | bytes 49156
  371.9 2.0 collective-permute-start
  374.1 14.9 %collective-permute-start.1 = (bf16[2,32,4096]{2,1,0:T(8,128)(2,1)S(1)}, bf16[2,32,4096]{2,1,0:T(8,128)(2,1)S(1)}, u32[]{:S(2)}, u32[]{:S(2)}) collective-permute-start(bf16[2,32,4096]{2,1,0:T(8,128)(2,1)S(1)} %fusion.36), channel_id=1, source_target_pairs={{0,2},{1,3},{4,6},{5,7},{8,10},{9,11},{12,14},{13,15},{16,18},{17,... | collective-permute-start | bytes 1572872 | tf_op jit(solution)/shard_map/ppermute | solution.py:309
  377.6 22.0 %all-gather.7.cloned.1.call-start = ((), (), s32[]{:S(2)}) async-start(), calls=%async_computation | async-start | bytes 1572864 | tf_op jit(solution)/shard_map/all_gather | solution.py:277
  390.3 69.3 %all-gather.9.cloned.1.call-start = ((), (), s32[]{:S(2)}) async-start(), calls=%async_computation.1 | async-start | bytes 1572864 | tf_op jit(solution)/shard_map/all_gather | solution.py:277
  399.6 6.7 %slice-start = ((s8[8388608]{0:T(1024)(128)(4,1)}), s8[4194304]{0:T(1024)(128)(4,1)S(1)}, s32[]{:S(2)}) async-start(s8[8388608]{0:T(1024)(128)(4,1)} %bitcast.145), calls=%async_computation.4 | async-start | bytes 8388608
  401.5 4.9 slice-start.1
  429.8 18.5 %copy-start.3 = (bf16[1,2,32,4096]{3,2,1,0:T(8,128)(2,1)S(1)}, bf16[1,2,32,4096]{3,2,1,0:T(8,128)(2,1)}, u32[]{:S(2)}) copy-start(bf16[1,2,32,4096]{3,2,1,0:T(8,128)(2,1)} %param.21) | copy-start | bytes 1572868
  429.8 2.0 collective-permute-start.3
  431.9 15.9 %collective-permute-start.4 = (bf16[2,32,4096]{2,1,0:T(8,128)(2,1)S(1)}, bf16[2,32,4096]{2,1,0:T(8,128)(2,1)S(1)}, u32[]{:S(2)}, u32[]{:S(2)}) collective-permute-start(bf16[2,32,4096]{2,1,0:T(8,128)(2,1)S(1)} %fusion.40), channel_id=1, source_target_pairs={{2,0},{3,1},{6,4},{7,5},{10,8},{11,9},{14,12},{15,13},{18,16},{19,... | collective-permute-start | bytes 1572872 | tf_op jit(solution)/shard_map/ppermute | solution.py:330
  456.7 34.5 %collective-permute-start.2 = (bf16[2,32,4096]{2,1,0:T(8,128)(2,1)}, bf16[2,32,4096]{2,1,0:T(8,128)(2,1)}, u32[]{:S(2)}, u32[]{:S(2)}) collective-permute-start(bf16[2,32,4096]{2,1,0:T(8,128)(2,1)} %dynamic-slice_bitcast_fusion.2), channel_id=1, source_target_pairs={{0,1},{1,0},{2,3},{3,2},{4,5},{5,4},{6,7},{7,6},{8,9},{9,8},{10,11... | collective-permute-start | bytes 1572872 | tf_op jit(solution)/shard_map/ppermute | solution.py:252
  474.4 13.1 %slice-start.2 = ((s8[8388608]{0:T(1024)(128)(4,1)}), s8[4194304]{0:T(1024)(128)(4,1)S(1)}, s32[]{:S(2)}) async-start(s8[8388608]{0:T(1024)(128)(4,1)} %bitcast.147), calls=%async_computation.6 | async-start | bytes 8388608
  481.0 6.5 %slice-start.3 = ((s8[8388608]{0:T(1024)(128)(4,1)}), s8[4194304]{0:T(1024)(128)(4,1)S(1)}, s32[]{:S(2)}) async-start(s8[8388608]{0:T(1024)(128)(4,1)} %bitcast.147), calls=%async_computation.7 | async-start | bytes 8388608
  491.0 2.3 collective-permute-start.6
  493.3 4.0 collective-permute-start.7
  497.4 4.0 collective-permute-start.8
  499.3 7.6 %copy-start.2 = (bf16[2,32,4096]{2,1,0:T(8,128)(2,1)S(1)}, bf16[2,32,4096]{2,1,0:T(8,128)(2,1)}, u32[]{:S(2)}) copy-start(bf16[2,32,4096]{2,1,0:T(8,128)(2,1)} %bitcast_select_fusion.1) | copy-start | bytes 1572868
  501.4 4.9 collective-permute-start.9
  504.2 2.7 collective-permute-start.5
  (7 other events, 18.5 us)
Sparse Core Ops, SparseCore 0:
  10.1 11.7 all-gather.10
  377.7 7.2 all-gather.12
  390.4 9.1 all-gather.6
  449.8 9.7 all-gather.8

commit v3 on v2

--- a/solution.py
+++ b/solution.py
@@ -97,14 +97,22 @@
     def sent(copy):
         copy.wait_send()
 
+    def begin_across(w, p):
+        across(w, p, a, b, own(w, p)).start()
+
+    def begin_along(w, p):
+        both_ways(w, p, a, b, own(w, p), start)
+
     def begin(w, p):
-        across(w, p, a, b, own(w, p)).start()
-        both_ways(w, p, a, b, own(w, p), start)
-
-    for w in range(4):
-        each(split, full, w, functools.partial(begin, w))
+        begin_along(w, p)
+        begin_across(w, p)
+
+    for w in range(4):
+        each(split, full, w, functools.partial(begin_across, w))
     for w in range(4):
         each(none, split, w, functools.partial(begin, w))
+    for w in range(4):
+        each(split, full, w, functools.partial(begin_along, w))
     for w in range(4):
         each(none, full, w, lambda p, w=w: pltpu.make_async_copy(
             own(w, p), slot(w, a, b, p), local_sem.at[w * parts + p]).start())
@@ -145,12 +153,13 @@
 
     def hop(dist, op):
         for w in range(4):
+            each(none, split, w, lambda p, w=w: relay(w, p, dist, b, True, op))
+        for w in range(4):
             def crossed_part(p, w=w):
                 relay(w, p, dist, b, False, op)
                 relay(w, p, dist, 1 - b, False, op)
 
             each(split, full, w, crossed_part)
-            each(none, split, w, lambda p, w=w: relay(w, p, dist, b, True, op))
 
     def hop_start(dist, c):
         hop(dist, start)

time: 515 us -> 509 us (0.988)
  Pallas kernels: 339 us -> 332 us
    pallas_call x1, Pallas kernels: 339 us -> 332 us  [gather_weights(): pl.pallas_call(functools.partial(gather_kernel, lines, parts, crossed), o...]
  transfers between devices with their start and end apart: 14 -> 14, of which waited for: 9 -> 9; matrix products, arithmetic and copies ran while one was open for 10% -> 10% of each run, Pallas kernels for 66% -> 65%
where the time goes in v3:
time: 509 us; the launch traced here: 508 us
  Pallas kernels  332 us (65%)
  matrix products  83.8 us (16%)
  waiting for transfers between devices  40.6 us (8%)
  other arithmetic  15.3 us (3%)
  between operations  14.4 us (3%)
  starting transfers between devices  12.6 us (2%)
  local copies, waits for them, and re-layouts  10 us (2%)
    pallas_call x1, Pallas kernels, gather_weights(): pl.pallas_call(functools.partial(gather_kernel, lines, parts, crossed), o...  332 us
    dot_general x7, matrix products, dot_t(): lax.dot_general(left, right, (((1,), (1,)), ((), ())), preferred_element_...  41.3 us
    dot_general x7, matrix products, dot(): return jnp.dot(left, right, preferred_element_type=jnp.float32)  29.5 us
    ppermute x1, waiting for transfers between devices, shards(): cross_sent = lax.ppermute(cross.astype(jnp.bfloat16), 'section', [(1, 0)])  14.4 us
    dot_general x11, matrix products, heads_einsum(): return jnp.einsum(spec, left, right, preferred_element_type=jnp.float32)  13 us
    ppermute x1, waiting for transfers between devices, shards(): from_enc = lax.ppermute(enc_out, 'section', [(0, 1)])  11.4 us
  transfers between devices with their start and end apart: 14, of which 9 were waited for; matrix products, arithmetic and copies ran while one was open for 10% of the time, Pallas kernels for 65%

profile of v3, /device:TPU:0, one launch (start us, length us, event | category | flops | bytes accessed | tf_op | source)
XLA Modules:
  0.0 508.4 jit_solution(16209340595333539731)
XLA Ops:
  9.6 331.7 %shard_map.138 = (bf16[4096,1024]{1,0:T(8,128)(2,1)}, bf16[4096,1024]{1,0:T(8,128)(2,1)}, bf16[4096,1024]{1,0:T(8,128)(2,1)}, bf16[1024,4096]{1,0:T(8,128)(2,1)}) custom-call(bf16[512,1024]{1,0:T(8,128)(2,1)} %bitcast.168, bf16[512,1024]{1,0:T(8,128)(2,1)} %bitcast.169, bf16[512,1024]{1,0:T(8,128)(2,1)} %bitcast.170, bf16[1024,512]{1,0:T(8,128)(2,1)} %bitcast.171), custom_call_target="tpu_custom_call" | custom-call | tf_op jit(solution)/shard_map/pallas_call | solution.py:205
  344.7 4.6 convolution_convert_fusion.14
  349.6 4.7 convolution_convert_fusion.15
  354.3 4.6 convolution_convert_fusion.13
  360.2 4.7 convolution_convert_fusion.1
  367.2 3.4 collective-permute-start.1
  370.7 11.4 %collective-permute-done.1 = bf16[2,32,4096]{2,1,0:T(8,128)(2,1)S(1)} collective-permute-done((bf16[2,32,4096]{2,1,0:T(8,128)(2,1)S(1)}, bf16[2,32,4096]{2,1,0:T(8,128)(2,1)S(1)}, u32[]{:S(2)}, u32[]{:S(2)}) %collective-permute-start.1) | collective-permute-done | bytes 524320 | tf_op jit(solution)/shard_map/ppermute | solution.py:318
  383.6 5.9 %fusion.28 = bf16[128,1024]{0,1:T(8,128)(2,1)S(1)} fusion(bf16[1024,4096]{1,0:T(8,128)(2,1)} %get-tuple-element.11, bf16[128,4096]{1,0:T(8,128)(2,1)} %bitcast.191), kind=kOutput, calls=%fused_computation.60 | convolution fusion | flops 1073872896 | bytes 9699328 | tf_op jit(solution)/shard_map/dot_general | solution.py:242
  390.8 2.8 all-gather.7.cloned.1.call-done
  395.5 4.9 convolution_convert_fusion.10
  407.7 2.1 fusion.14
  411.3 6.2 %fusion.84 = f32[128,4096]{1,0:T(8,128)S(1)} fusion(bf16[128,1024]{1,0:T(8,128)(2,1)S(1)} %bitcast.172, bf16[4096,1024]{1,0:T(8,128)(2,1)} %get-tuple-element.10), kind=kOutput, calls=%fused_computation.140 | convolution fusion | flops 1073741824 | bytes 10747904 | tf_op jit(solution)/shard_map/dot_general | solution.py:242
  417.5 6.3 %fusion.6 = bf16[128,4096]{1,0:T(8,128)(2,1)S(1)} fusion(f32[128,4096]{1,0:T(8,128)S(1)} %fusion.84, bf16[128,1024]{1,0:T(8,128)(2,1)S(1)} %bitcast.160, bf16[4096,1024]{1,0:T(8,128)(2,1)} %get-tuple-element.8), kind=kOutput, calls=%fused_computation.8 | convolution fusion | flops 1074790400 | bytes 11796480 | tf_op jit(solution)/shard_map/dot_general | solution.py:242
  427.5 14.4 %collective-permute-done.4 = bf16[2,32,4096]{2,1,0:T(8,128)(2,1)S(1)} collective-permute-done((bf16[2,32,4096]{2,1,0:T(8,128)(2,1)S(1)}, bf16[2,32,4096]{2,1,0:T(8,128)(2,1)S(1)}, u32[]{:S(2)}, u32[]{:S(2)}) %collective-permute-start.4) | collective-permute-done | bytes 524320 | tf_op jit(solution)/shard_map/ppermute | solution.py:339
  445.2 4.7 convolution_convert_fusion
  450.7 2.8 all-gather.9.cloned.1.call-done
  453.5 6.6 %convolution_convert_fusion.7 = bf16[128,1024]{1,0:T(8,128)(2,1)S(1)} fusion(bf16[128,4096]{1,0:T(8,128)(2,1)} %bitcast.159, bf16[1024,4096]{1,0:T(8,128)(2,1)} %get-tuple-element.11), kind=kOutput, calls=%fused_computation.32 | convolution fusion | flops 1073872896 | bytes 9699328 | tf_op jit(solution)/shard_map/dot_general | solution.py:242
  460.6 2.0 fusion.17
  468.4 6.4 %fusion.86 = f32[128,4096]{1,0:T(8,128)S(1)} fusion(bf16[128,1024]{1,0:T(8,128)(2,1)S(1)} %bitcast.173, bf16[4096,1024]{1,0:T(8,128)(2,1)} %get-tuple-element.10), kind=kOutput, calls=%fused_computation.142 | convolution fusion | flops 1073741824 | bytes 10747904 | tf_op jit(solution)/shard_map/dot_general | solution.py:242
  475.1 6.4 %fusion.85 = f32[128,4096]{1,0:T(8,128)S(1)} fusion(bf16[128,1024]{1,0:T(8,128)(2,1)S(1)} %bitcast.174, bf16[4096,1024]{1,0:T(8,128)(2,1)} %get-tuple-element.9), kind=kOutput, calls=%fused_computation.141 | convolution fusion | flops 1073741824 | bytes 10747904 | tf_op jit(solution)/shard_map/dot_general | solution.py:242
  481.5 3.4 multiply_reduce_fusion.1
  485.3 2.0 fusion.42
  489.2 2.1 collective-permute-done.7
  495.4 2.8 collective-permute-start.9
  (128 shorter events, 47.0 us)
Async XLA Ops:
  7.2 334.4 %all-gather.11.cloned.1.call-start = ((), (), s32[]{:S(2)}) async-start(), calls=%async_computation.2 | async-start | bytes 1572864 | tf_op jit(solution)/shard_map/all_gather | solution.py:286
  9.2 374.4 %all-gather.13.cloned.1.call-start = ((), (), s32[]{:S(2)}) async-start(), calls=%async_computation.3 | async-start | bytes 1572864 | tf_op jit(solution)/shard_map/all_gather | solution.py:286
  9.6 333.6 %copy-start.10 = (f32[1,4096]{1,0:T(1,128)S(1)}, f32[1,4096]{1,0:T(1,128)}, u32[]{:S(2)}) copy-start(f32[1,4096]{1,0:T(1,128)} %param.19) | copy-start | bytes 49156
  349.6 9.8 %copy-start.5 = (bf16[2,64,4,256]{3,2,1,0:T(4,128)(2,1)}, bf16[2,64,4,256]{3,2,1,0:T(4,128)(2,1)S(1)}, u32[]{:S(2)}) copy-start(bf16[2,64,4,256]{3,2,1,0:T(4,128)(2,1)S(1)} %reshape.134) | copy-start | bytes 786436
  360.2 6.8 %copy-start.1 = (bf16[1,2,32,4096]{3,2,1,0:T(8,128)(2,1)S(1)}, bf16[1,2,32,4096]{3,2,1,0:T(8,128)(2,1)}, u32[]{:S(2)}) copy-start(bf16[1,2,32,4096]{3,2,1,0:T(8,128)(2,1)} %broadcast_select_fusion.2) | copy-start | bytes 1572868
  365.0 17.3 %copy-start.9 = (f32[4096]{0:T(1024)S(1)}, f32[4096]{0:T(1024)}, u32[]{:S(2)}) copy-start(f32[4096]{0:T(1024)} %param.20) | copy-start | bytes 49156
  365.0 2.0 collective-permute-start
  367.2 14.9 %collective-permute-start.1 = (bf16[2,32,4096]{2,1,0:T(8,128)(2,1)S(1)}, bf16[2,32,4096]{2,1,0:T(8,128)(2,1)S(1)}, u32[]{:S(2)}, u32[]{:S(2)}) collective-permute-start(bf16[2,32,4096]{2,1,0:T(8,128)(2,1)S(1)} %fusion.36), channel_id=1, source_target_pairs={{0,2},{1,3},{4,6},{5,7},{8,10},{9,11},{12,14},{13,15},{16,18},{17,... | collective-permute-start | bytes 1572872 | tf_op jit(solution)/shard_map/ppermute | solution.py:318
  370.6 23.0 %all-gather.7.cloned.1.call-start = ((), (), s32[]{:S(2)}) async-start(), calls=%async_computation | async-start | bytes 1572864 | tf_op jit(solution)/shard_map/all_gather | solution.py:286
  383.3 70.2 %all-gather.9.cloned.1.call-start = ((), (), s32[]{:S(2)}) async-start(), calls=%async_computation.1 | async-start | bytes 1572864 | tf_op jit(solution)/shard_map/all_gather | solution.py:286
  393.6 6.7 %slice-start = ((s8[8388608]{0:T(1024)(128)(4,1)}), s8[4194304]{0:T(1024)(128)(4,1)S(1)}, s32[]{:S(2)}) async-start(s8[8388608]{0:T(1024)(128)(4,1)} %bitcast.145), calls=%async_computation.4 | async-start | bytes 8388608
  395.5 4.9 slice-start.1
  423.8 18.5 %copy-start.3 = (bf16[1,2,32,4096]{3,2,1,0:T(8,128)(2,1)S(1)}, bf16[1,2,32,4096]{3,2,1,0:T(8,128)(2,1)}, u32[]{:S(2)}) copy-start(bf16[1,2,32,4096]{3,2,1,0:T(8,128)(2,1)} %param.21) | copy-start | bytes 1572868
  423.8 2.0 collective-permute-start.3
  425.9 15.9 %collective-permute-start.4 = (bf16[2,32,4096]{2,1,0:T(8,128)(2,1)S(1)}, bf16[2,32,4096]{2,1,0:T(8,128)(2,1)S(1)}, u32[]{:S(2)}, u32[]{:S(2)}) collective-permute-start(bf16[2,32,4096]{2,1,0:T(8,128)(2,1)S(1)} %fusion.40), channel_id=1, source_target_pairs={{2,0},{3,1},{6,4},{7,5},{10,8},{11,9},{14,12},{15,13},{18,16},{19,... | collective-permute-start | bytes 1572872 | tf_op jit(solution)/shard_map/ppermute | solution.py:339
  450.7 34.5 %collective-permute-start.2 = (bf16[2,32,4096]{2,1,0:T(8,128)(2,1)}, bf16[2,32,4096]{2,1,0:T(8,128)(2,1)}, u32[]{:S(2)}, u32[]{:S(2)}) collective-permute-start(bf16[2,32,4096]{2,1,0:T(8,128)(2,1)} %dynamic-slice_bitcast_fusion.2), channel_id=1, source_target_pairs={{0,1},{1,0},{2,3},{3,2},{4,5},{5,4},{6,7},{7,6},{8,9},{9,8},{10,11... | collective-permute-start | bytes 1572872 | tf_op jit(solution)/shard_map/ppermute | solution.py:261
  468.4 13.1 %slice-start.2 = ((s8[8388608]{0:T(1024)(128)(4,1)}), s8[4194304]{0:T(1024)(128)(4,1)S(1)}, s32[]{:S(2)}) async-start(s8[8388608]{0:T(1024)(128)(4,1)} %bitcast.147), calls=%async_computation.6 | async-start | bytes 8388608
  475.0 6.5 %slice-start.3 = ((s8[8388608]{0:T(1024)(128)(4,1)}), s8[4194304]{0:T(1024)(128)(4,1)S(1)}, s32[]{:S(2)}) async-start(s8[8388608]{0:T(1024)(128)(4,1)} %bitcast.147), calls=%async_computation.7 | async-start | bytes 8388608
  485.0 2.3 collective-permute-start.6
  487.3 4.0 collective-permute-start.7
  491.4 4.0 collective-permute-start.8
  493.3 7.6 %copy-start.2 = (bf16[2,32,4096]{2,1,0:T(8,128)(2,1)S(1)}, bf16[2,32,4096]{2,1,0:T(8,128)(2,1)}, u32[]{:S(2)}) copy-start(bf16[2,32,4096]{2,1,0:T(8,128)(2,1)} %bitcast_select_fusion.1) | copy-start | bytes 1572868
  495.4 4.9 collective-permute-start.9
  498.2 2.7 collective-permute-start.5
  (7 other events, 19.5 us)
Sparse Core Ops, SparseCore 0:
  10.1 11.7 all-gather.10
  370.8 8.1 all-gather.12
  383.5 10.1 all-gather.6
  443.8 9.7 all-gather.8

commit v4 on v3

--- a/solution.py
+++ b/solution.py
@@ -261,6 +261,10 @@
     return lax.ppermute(array, axis, [(0, 1), (1, 0)])
 
 
+def after(array, other):
+    return array + (0.0 * other[0, 0].astype(jnp.float32)).astype(array.dtype)
+
+
 def sum_of_all(array):
     array = array + partner(array, "mp")
     count = lax.axis_size("dp")
@@ -312,18 +316,19 @@
         mixed = heads_einsum("mhqk,mkhd->mqhd", attention.astype(jnp.bfloat16), value)
         part = dot(mixed.astype(jnp.bfloat16).reshape(rows, -1), full_o)
         result = (entry.astype(jnp.float32) + add_pieces(part)).astype(jnp.bfloat16)
-        return result, key, value, attention
+        return result, key, value, attention, part
 
     enc_out = forward(hidden)[0]
-    from_enc = lax.ppermute(enc_out, "section", [(0, 1)])
+    mixed_last = dot_t(grad_last, full_o).astype(jnp.bfloat16)
+    from_enc = after(lax.ppermute(enc_out, "section", [(0, 1)]), mixed_last)
     encoded = jnp.where(is_encoder, enc_out, from_enc)
     normed, enc_normal, enc_spread = rms_norm(encoded, final_gain)
     source = jnp.where(is_encoder, hidden, all_rows(normed.astype(jnp.bfloat16)))
-    layer_out, key, value, attention = forward(source)
+    layer_out, key, value, attention, last_part = forward(source)
     attention_b = attention.astype(jnp.bfloat16)
 
-    def score_grads(grad_rows):
-        grad_mixed = heads_of(dot_t(grad_rows, full_o).astype(jnp.bfloat16), micro)
+    def score_grads(mixed_rows):
+        grad_mixed = heads_of(mixed_rows, micro)
         grad_value = heads_einsum("mhqk,mqhd->mkhd", attention_b, grad_mixed)
         grad_att = heads_einsum("mqhd,mkhd->mhqk", grad_mixed, value)
         shared = jnp.sum(attention * grad_att, axis=-1, keepdims=True)
@@ -335,15 +340,16 @@
         )
         return grad_scores, grad_source
 
-    cross = add_pieces(score_grads(grad_last)[1])
+    cross = add_pieces(score_grads(mixed_last)[1])
     cross_sent = lax.ppermute(cross.astype(jnp.bfloat16), "section", [(1, 0)])
+    cross_sent = after(cross_sent, last_part)
     cross = jnp.where(is_encoder, cross_sent, cross.astype(jnp.bfloat16)).astype(jnp.float32)
     enc_grads = norm_back(cross, enc_normal, enc_spread, final_gain).astype(jnp.bfloat16)
     final_part = jnp.sum(cross * enc_normal, axis=(0, 1))
 
     grad_piece = jnp.where(is_encoder, enc_grads, cotangent[0])
     grad_rows = all_rows(grad_piece)
-    grad_scores, grad_source = score_grads(grad_rows)
+    grad_scores, grad_source = score_grads(dot_t(grad_rows, full_o).astype(jnp.bfloat16))
     grad_query = heads_einsum("mhqk,mkhd->mqhd", grad_scores, key)
     grad_hidden = dot_t(grad_query.astype(jnp.bfloat16).reshape(rows, -1), full_q)
     grad_hidden = grad_hidden + jnp.where(is_encoder, grad_source, 0.0)

time: 509 us -> 513 us (level)
    all_gather x4, waiting for transfers between devices: 5.64 us -> 21 us  [all_rows(): return lax.all_gather(pieces, 'mp', axis=1, tiled=True).reshape(rows, width)]
    ppermute x1, waiting for transfers between devices: 11.4 us -> 0.38 us  [shards(): from_enc = after(lax.ppermute(enc_out, 'section', [(0, 1)]), mixed_last)]
    ppermute x1, waiting for transfers between devices: 14.4 us -> 7.69 us  [shards(): cross_sent = lax.ppermute(cross.astype(jnp.bfloat16), 'section', [(1, 0)])]
where the time goes in v4:
time: 513 us; the launch traced here: 512 us
  Pallas kernels  332 us (65%)
  matrix products  86.2 us (17%)
  waiting for transfers between devices  36.5 us (7%)
  between operations  15.7 us (3%)
  other arithmetic  15.5 us (3%)
  local copies, waits for them, and re-layouts  14 us (3%)
  starting transfers between devices  12.6 us (2%)
    pallas_call x1, Pallas kernels, gather_weights(): pl.pallas_call(functools.partial(gather_kernel, lines, parts, crossed), o...  332 us
    dot_general x7, matrix products, dot_t(): lax.dot_general(left, right, (((1,), (1,)), ((), ())), preferred_element_...  41.3 us
    dot_general x7, matrix products, dot(): return jnp.dot(left, right, preferred_element_type=jnp.float32)  30.5 us
    all_gather x4, waiting for transfers between devices, all_rows(): return lax.all_gather(pieces, 'mp', axis=1, tiled=True).reshape(rows, width)  21 us
    dot_general x11, matrix products, heads_einsum(): return jnp.einsum(spec, left, right, preferred_element_type=jnp.float32)  14.5 us
  transfers between devices with their start and end apart: 14, of which 9 were waited for; matrix products, arithmetic and copies ran while one was open for 10% of the time, Pallas kernels for 65%

profile of v4, /device:TPU:0, one launch (start us, length us, event | category | flops | bytes accessed | tf_op | source)
XLA Modules:
  0.0 512.2 jit_solution(5265515159403389643)
XLA Ops:
  9.6 331.7 %shard_map.138 = (bf16[4096,1024]{1,0:T(8,128)(2,1)}, bf16[4096,1024]{1,0:T(8,128)(2,1)}, bf16[4096,1024]{1,0:T(8,128)(2,1)}, bf16[1024,4096]{1,0:T(8,128)(2,1)}) custom-call(bf16[512,1024]{1,0:T(8,128)(2,1)} %bitcast.171, bf16[512,1024]{1,0:T(8,128)(2,1)} %bitcast.172, bf16[512,1024]{1,0:T(8,128)(2,1)} %bitcast.173, bf16[1024,512]{1,0:T(8,128)(2,1)} %bitcast.174), custom_call_target="tpu_custom_call" | custom-call | tf_op jit(solution)/shard_map/pallas_call | solution.py:205
  344.7 4.6 convolution_convert_fusion.13
  349.6 4.7 convolution_convert_fusion.14
  354.3 4.6 convolution_convert_fusion.12
  360.2 4.7 convolution_convert_fusion
  367.2 3.6 collective-permute-start.1
  370.8 3.7 all-gather.13.cloned.1.call-done
  374.5 5.9 %fusion.28 = bf16[128,1024]{0,1:T(8,128)(2,1)S(1)} fusion(bf16[1024,4096]{1,0:T(8,128)(2,1)} %get-tuple-element.11, bf16[128,4096]{1,0:T(8,128)(2,1)} %bitcast.194), kind=kOutput, calls=%fused_computation.59 | convolution fusion | flops 1073872896 | bytes 9699328 | tf_op jit(solution)/shard_map/dot_general | solution.py:242
  384.7 9.0 %all-gather.7.cloned.1.call-done = bf16[2,64,4096]{2,1,0:T(8,128)(2,1)} async-done(((bf16[2,32,4096]{2,1,0:T(8,128)(2,1)}), bf16[2,64,4096]{2,1,0:T(8,128)(2,1)}) %all-gather.7.cloned.1.call-update) | async-done | bytes 1048592 | tf_op jit(solution)/shard_map/all_gather | solution.py:290
  395.5 4.9 convolution_convert_fusion.8
  407.7 2.1 fusion.14
  411.3 6.2 %fusion.85 = f32[128,4096]{1,0:T(8,128)S(1)} fusion(bf16[128,1024]{1,0:T(8,128)(2,1)S(1)} %bitcast.175, bf16[4096,1024]{1,0:T(8,128)(2,1)} %get-tuple-element.10), kind=kOutput, calls=%fused_computation.140 | convolution fusion | flops 1073741824 | bytes 10747904 | tf_op jit(solution)/shard_map/dot_general | solution.py:242
  417.5 6.3 %fusion.6 = bf16[128,4096]{1,0:T(8,128)(2,1)S(1)} fusion(f32[128,4096]{1,0:T(8,128)S(1)} %fusion.85, bf16[128,1024]{1,0:T(8,128)(2,1)S(1)} %bitcast.163, bf16[4096,1024]{1,0:T(8,128)(2,1)} %get-tuple-element.8), kind=kOutput, calls=%fused_computation.8 | convolution fusion | flops 1074790400 | bytes 11796480 | tf_op jit(solution)/shard_map/dot_general | solution.py:242
  431.7 5.6 %fusion.84 = (bf16[128,4096]{1,0:T(8,128)(2,1)}, f32[128,4096]{1,0:T(8,128)S(1)}) fusion(bf16[128,1024]{1,0:T(8,128)(2,1)S(1)} %bitcast.161, bf16[1024,4096]{1,0:T(8,128)(2,1)} %get-tuple-element.11), kind=kOutput, calls=%fused_computation.139 | convolution fusion | flops 1074266112 | bytes 11796480 | tf_op jit(solution)/shard_map/dot_general | solution.py:238
  438.6 7.7 %collective-permute-done.4 = bf16[2,32,4096]{2,1,0:T(8,128)(2,1)S(1)} collective-permute-done((bf16[2,32,4096]{2,1,0:T(8,128)(2,1)S(1)}, bf16[2,32,4096]{2,1,0:T(8,128)(2,1)S(1)}, u32[]{:S(2)}, u32[]{:S(2)}) %collective-permute-start.4) | collective-permute-done | bytes 524320 | tf_op jit(solution)/shard_map/ppermute | solution.py:344
  449.3 8.3 %all-gather.9.cloned.1.call-done = bf16[2,64,4096]{2,1,0:T(8,128)(2,1)} async-done(((bf16[2,32,4096]{2,1,0:T(8,128)(2,1)}), bf16[2,64,4096]{2,1,0:T(8,128)(2,1)}) %all-gather.9.cloned.1.call-update) | async-done | bytes 1048592 | tf_op jit(solution)/shard_map/all_gather | solution.py:290
  457.6 6.6 %convolution_convert_fusion.6 = bf16[128,1024]{1,0:T(8,128)(2,1)S(1)} fusion(bf16[128,4096]{1,0:T(8,128)(2,1)} %bitcast.162, bf16[1024,4096]{1,0:T(8,128)(2,1)} %get-tuple-element.11), kind=kOutput, calls=%fused_computation.31 | convolution fusion | flops 1073872896 | bytes 9699328 | tf_op jit(solution)/shard_map/dot_general | solution.py:242
  464.6 2.0 fusion.17
  466.6 2.1 fusion.13
  473.2 6.4 %fusion.87 = f32[128,4096]{1,0:T(8,128)S(1)} fusion(bf16[128,1024]{1,0:T(8,128)(2,1)S(1)} %bitcast.176, bf16[4096,1024]{1,0:T(8,128)(2,1)} %get-tuple-element.10), kind=kOutput, calls=%fused_computation.142 | convolution fusion | flops 1073741824 | bytes 10747904 | tf_op jit(solution)/shard_map/dot_general | solution.py:242
  479.9 6.4 %fusion.86 = f32[128,4096]{1,0:T(8,128)S(1)} fusion(bf16[128,1024]{1,0:T(8,128)(2,1)S(1)} %bitcast.177, bf16[4096,1024]{1,0:T(8,128)(2,1)} %get-tuple-element.9), kind=kOutput, calls=%fused_computation.141 | convolution fusion | flops 1073741824 | bytes 10747904 | tf_op jit(solution)/shard_map/dot_general | solution.py:242
  486.3 3.4 multiply_reduce_fusion.1
  493.0 2.1 collective-permute-done.7
  499.1 2.8 collective-permute-start.9
  (136 shorter events, 50.9 us)
Async XLA Ops:
  7.2 334.4 %all-gather.11.cloned.1.call-start = ((), (), s32[]{:S(2)}) async-start(), calls=%async_computation.2 | async-start | bytes 1572864 | tf_op jit(solution)/shard_map/all_gather | solution.py:290
  9.2 365.4 %all-gather.13.cloned.1.call-start = ((), (), s32[]{:S(2)}) async-start(), calls=%async_computation.3 | async-start | bytes 1572864 | tf_op jit(solution)/shard_map/all_gather | solution.py:290
  9.6 333.6 %copy-start.13 = (f32[1,4096]{1,0:T(1,128)S(1)}, f32[1,4096]{1,0:T(1,128)}, u32[]{:S(2)}) copy-start(f32[1,4096]{1,0:T(1,128)} %param.19) | copy-start | bytes 49156
  349.6 9.8 %copy-start.7 = (bf16[2,64,4,256]{3,2,1,0:T(4,128)(2,1)}, bf16[2,64,4,256]{3,2,1,0:T(4,128)(2,1)S(1)}, u32[]{:S(2)}) copy-start(bf16[2,64,4,256]{3,2,1,0:T(4,128)(2,1)S(1)} %reshape.141) | copy-start | bytes 786436
  360.2 6.8 %copy-start.1 = (bf16[1,2,32,4096]{3,2,1,0:T(8,128)(2,1)S(1)}, bf16[1,2,32,4096]{3,2,1,0:T(8,128)(2,1)}, u32[]{:S(2)}) copy-start(bf16[1,2,32,4096]{3,2,1,0:T(8,128)(2,1)} %broadcast_select_fusion) | copy-start | bytes 1572868
  365.0 2.0 collective-permute-start
  365.1 28.6 %all-gather.7.cloned.1.call-start = ((), (), s32[]{:S(2)}) async-start(), calls=%async_computation | async-start | bytes 1572864 | tf_op jit(solution)/shard_map/all_gather | solution.py:290
  367.2 14.9 %collective-permute-start.1 = (bf16[2,32,4096]{2,1,0:T(8,128)(2,1)S(1)}, bf16[2,32,4096]{2,1,0:T(8,128)(2,1)S(1)}, u32[]{:S(2)}, u32[]{:S(2)}) collective-permute-start(bf16[2,32,4096]{2,1,0:T(8,128)(2,1)S(1)} %fusion.36), channel_id=1, source_target_pairs={{0,2},{1,3},{4,6},{5,7},{8,10},{9,11},{12,14},{13,15},{16,18},{17,... | collective-permute-start | bytes 1572872 | tf_op jit(solution)/shard_map/ppermute | solution.py:323
  374.5 7.8 %copy-start.12 = (f32[4096]{0:T(1024)S(1)}, f32[4096]{0:T(1024)}, u32[]{:S(2)}) copy-start(f32[4096]{0:T(1024)} %param.20) | copy-start | bytes 49156
  382.3 11.3 %copy-start = (bf16[1,2,64,4096]{3,2,1,0:T(8,128)(2,1)S(1)}, bf16[1,2,64,4096]{3,2,1,0:T(8,128)(2,1)}, u32[]{:S(2)}) copy-start(bf16[1,2,64,4096]{3,2,1,0:T(8,128)(2,1)} %all-gather.11.cloned.1.call-done) | copy-start | bytes 3145732
  383.4 74.2 %all-gather.9.cloned.1.call-start = ((), (), s32[]{:S(2)}) async-start(), calls=%async_computation.1 | async-start | bytes 1572864 | tf_op jit(solution)/shard_map/all_gather | solution.py:290
  393.7 6.7 %slice-start = ((s8[8388608]{0:T(1024)(128)(4,1)}), s8[4194304]{0:T(1024)(128)(4,1)S(1)}, s32[]{:S(2)}) async-start(s8[8388608]{0:T(1024)(128)(4,1)} %bitcast.148), calls=%async_computation.4 | async-start | bytes 8388608
  425.6 3.4 collective-permute-start.3
  430.2 16.0 %collective-permute-start.4 = (bf16[2,32,4096]{2,1,0:T(8,128)(2,1)S(1)}, bf16[2,32,4096]{2,1,0:T(8,128)(2,1)S(1)}, u32[]{:S(2)}, u32[]{:S(2)}) collective-permute-start(bf16[2,32,4096]{2,1,0:T(8,128)(2,1)S(1)} %fusion.40), channel_id=1, source_target_pairs={{2,0},{3,1},{6,4},{7,5},{10,8},{11,9},{14,12},{15,13},{18,16},{19,... | collective-permute-start | bytes 1572872 | tf_op jit(solution)/shard_map/ppermute | solution.py:344
  437.4 9.4 %copy-start.5 = (bf16[1,2,32,4096]{3,2,1,0:T(8,128)(2,1)S(1)}, bf16[1,2,32,4096]{3,2,1,0:T(8,128)(2,1)}, u32[]{:S(2)}) copy-start(bf16[1,2,32,4096]{3,2,1,0:T(8,128)(2,1)} %param.21) | copy-start | bytes 1572868
  449.2 40.8 %collective-permute-start.2 = (bf16[2,32,4096]{2,1,0:T(8,128)(2,1)S(1)}, bf16[2,32,4096]{2,1,0:T(8,128)(2,1)S(1)}, u32[]{:S(2)}, u32[]{:S(2)}) collective-permute-start(bf16[2,32,4096]{2,1,0:T(8,128)(2,1)S(1)} %dynamic-slice_bitcast_fusion.2), channel_id=1, source_target_pairs={{0,1},{1,0},{2,3},{3,2},{4,5},{5,4},{6,7},{7,6},{8,9},{9,8},{10,11... | collective-permute-start | bytes 1572872 | tf_op jit(solution)/shard_map/ppermute | solution.py:261
  473.2 13.1 %slice-start.2 = ((s8[8388608]{0:T(1024)(128)(4,1)}), s8[4194304]{0:T(1024)(128)(4,1)S(1)}, s32[]{:S(2)}) async-start(s8[8388608]{0:T(1024)(128)(4,1)} %bitcast.150), calls=%async_computation.6 | async-start | bytes 8388608
  479.8 6.4 %slice-start.3 = ((s8[8388608]{0:T(1024)(128)(4,1)}), s8[4194304]{0:T(1024)(128)(4,1)S(1)}, s32[]{:S(2)}) async-start(s8[8388608]{0:T(1024)(128)(4,1)} %bitcast.150), calls=%async_computation.7 | async-start | bytes 8388608
  489.8 1.3 collective-permute-start.6
  491.1 4.0 collective-permute-start.7
  495.1 4.0 collective-permute-start.8
  497.0 7.6 %copy-start.2 = (bf16[2,32,4096]{2,1,0:T(8,128)(2,1)S(1)}, bf16[2,32,4096]{2,1,0:T(8,128)(2,1)}, u32[]{:S(2)}) copy-start(bf16[2,32,4096]{2,1,0:T(8,128)(2,1)} %bitcast_select_fusion.1) | copy-start | bytes 1572868
  499.1 4.9 collective-permute-start.9
  502.0 2.7 collective-permute-start.5
  (10 other events, 32.2 us)
Sparse Core Ops, SparseCore 0:
  10.1 11.7 all-gather.10
  365.2 9.2 all-gather.12
  383.5 10.1 all-gather.6
  448.2 9.2 all-gather.8
